TPU v7x, 128 devices: a whole 4x4x4 slice. The times are simulated.
128 devices in a mesh: tg: 8 (over x, y_hi), pool: 16 (over y_lo, z, core).
Axes of the slice: x: 4, y: 4 (y_hi: 2, y_lo: 2; y = y_hi * 2 + y_lo), z: 4, core: 2. Of those that a mesh axis runs over, the one named last changes fastest.
Arguments:
- wave_coef: float32 [2, 64, 512, 128], P(None, 'pool', 'tg'), may hold values from -6 to 6
- potential: float32 [128, 128, 128], P('tg'), may hold values from -1 to 3
- stick_pos: int32 [512], replicated, may hold values from 0 to 16383, as said below
- stick_count: int32 [8], replicated, may hold values from 32 to 64, as said below
- ritz_block: float32 [2, 64, 4096], P(None, 'pool'), may hold values from -0.75 to 0.75
- slab_base: bfloat16 [2, 65536, 4096], P(None, ('tg', 'pool')), may hold values from -6 to 6
Outputs:
- applied: float32 [2, 64, 512, 128], P(None, 'pool', 'tg')
- rotated: bfloat16 [2, 65536, 4096], P(None, ('tg', 'pool'))
Inputs may be any that keep to these rules, and one draw needn't show every extreme that they name: `stick_pos`: distinct columns; both the first and the last column of the grid appear. `stick_count`: slots at or beyond this count on an index of tg are not in use; some index uses all 64 and some index half of them.
All inputs are finite; a program needn't handle non-finite values.
Results may differ from a plain program's by a relative error of at most 0.001.
Values sent between devices are 32-bit elements; how exact they have to be, the bound alone decides.
A program may use at most 128 MiB of HBM per device.

v0:
```python
import functools
import math

import jax
import jax.numpy as jnp
import ml_dtypes
import numpy as np
from jax import lax
from jax.experimental import pallas as pl
from jax.experimental.pallas import tpu as pltpu
from jax.sharding import PartitionSpec as P

NX = 128
NY = 128
BF16 = jnp.bfloat16
F32 = jnp.float32


def np_split(table):
    high = table.astype(np.float32).astype(ml_dtypes.bfloat16)
    low = (table - high.astype(np.float64)).astype(ml_dtypes.bfloat16)
    return high, low


def np_cs(length):
    idx = np.arange(length)
    ang = (idx[:, None] * idx[None, :] % length) * (2.0 * math.pi / length)
    return np.cos(ang), np.sin(ang)


def row_table(length, sign, scale=1.0):
    cos_t, sin_t = np_cs(length)
    return scale * np.block([[cos_t, sign * sin_t], [-sign * sin_t, cos_t]])


def split(values):
    high = values.astype(BF16)
    low = (values - high.astype(F32)).astype(BF16)
    return high, low


def as_rhs_rows(table):
    high, low = np_split(table)
    return np.concatenate([high, high, low], axis=0)


def as_lhs(table):
    high, low = np_split(table)
    return np.concatenate([high, high, low], axis=1)


def lanes3(values):
    high, low = split(values)
    return jnp.concatenate([high, low, high], axis=1)


def rows3(values):
    high, low = split(values)
    return jnp.concatenate([high, low, high], axis=0)


def dot(a, b):
    return lax.dot_general(a, b, (((1,), (0,)), ((), ())), preferred_element_type=F32)


def dot_nt(a, b):
    return lax.dot_general(a, b, (((1,), (1,)), ((), ())), preferred_element_type=F32)


def plane_kernel(pos_ref, sticks_ref, parity_ref, pot_ref, ty_ref, ax_ref, bx_ref, by_ref,
                 out_ref, grid_ref, re_ref, im_ref, gre_ref, gim_ref):
    slots = sticks_ref.shape[0]
    half = 64

    @pl.loop(0, 128)
    def _(x):
        grid_ref[pl.ds(pl.multiple_of(x * 128, 128), 128), :] = jnp.zeros((128, 128), F32)

    @pl.loop(0, slots // 8)
    def _(block):
        base = pl.multiple_of(block * 8, 8)
        rows = sticks_ref[pl.ds(base, 8), :]
        for k in range(8):
            grid_ref[pl.ds(pos_ref[base + k], 1), :] = rows[k:k + 1, :]

    @pl.loop(0, 64)
    def _(pair):
        parts = []
        for k in range(2):
            x = pair * 2 + k
            flipped = grid_ref[pl.ds(pl.multiple_of(x * 128, 128), 128), :].T
            parts.append(jnp.concatenate([flipped[:half], flipped[half:]], axis=1))
        res = dot(lanes3(jnp.concatenate(parts, axis=0)), ty_ref[...])
        at = pl.ds(pl.multiple_of(pair * 128, 128), 128)
        re_ref[at, :] = res[:, :128]
        im_ref[at, :] = res[:, 128:]

    @pl.loop(0, 16)
    def _(z):
        pot = pot_ref[z]
        for pair in range(2):
            at = [pl.ds((pair * 2 + k) * 16 + z, 128, half) for k in range(2)]
            data = jnp.concatenate(
                [jnp.concatenate([re_ref[a, :], im_ref[a, :]], axis=0) for a in at], axis=1)
            field = dot(ax_ref[...], rows3(data))
            wide = jnp.concatenate([pot, pot], axis=1)
            wide = jnp.concatenate([wide, wide], axis=0)
            back = dot(bx_ref[...], rows3(field * wide))
            for k in range(2):
                re_ref[at[k], :] = back[:128, k * 128:(k + 1) * 128]
                im_ref[at[k], :] = back[128:, k * 128:(k + 1) * 128]

    @pl.loop(0, 32)
    def _(group):
        at = pl.ds(pl.multiple_of(group * 256, 256), 256)
        data = jnp.concatenate([re_ref[at, :], im_ref[at, :]], axis=1)
        res = dot_nt(by_ref[...], lanes3(data))
        for k in range(2):
            to = pl.ds(pl.multiple_of((group * 2 + k) * 256, 256), 256)
            grid_ref[to, :] = res[:, k * 128:(k + 1) * 128]

    @pl.loop(0, slots // 8)
    def _(block):
        base = pl.multiple_of(block * 8, 8)
        for k in range(8):
            pos = pos_ref[base + k]
            row = (pos >> 8) * 256 + (pos & 127)
            gre_ref[pl.ds(base + k, 1), :] = grid_ref[pl.ds(row, 1), :]
            gim_ref[pl.ds(base + k, 1), :] = grid_ref[pl.ds(row + 128, 1), :]

    @pl.loop(0, slots // 64)
    def _(block):
        at = pl.ds(pl.multiple_of(block * 64, 64), 64)
        odd = jnp.broadcast_to(parity_ref[at, :], (64, half)) > 0
        gre = gre_ref[at, :]
        gim = gim_ref[at, :]
        out_ref[at, :] = jnp.concatenate(
            [jnp.where(odd, gre[:, half:], gre[:, :half]),
             jnp.where(odd, gim[:, half:], gim[:, :half])], axis=1)


def plane_step(sticks, stick_pos, pot):
    slots = sticks.shape[0]
    volume = 128.0 ** 3
    ty = as_rhs_rows(row_table(128, 1.0))
    ax = as_lhs(row_table(128, 1.0, 1.0 / volume).T)
    bx = as_lhs(row_table(128, -1.0).T)
    by = as_lhs(row_table(128, -1.0).T)
    parity = ((stick_pos >> 7) & 1).reshape(slots, 1)
    vmem = pl.BlockSpec(memory_space=pltpu.VMEM)
    return pl.pallas_call(
        plane_kernel,
        out_shape=jax.ShapeDtypeStruct((slots, 128), F32),
        in_specs=[pl.BlockSpec(memory_space=pltpu.SMEM)] + [vmem] * 7,
        out_specs=vmem,
        scratch_shapes=[
            pltpu.VMEM((16384, 128), F32),
            pltpu.VMEM((8192, 128), F32),
            pltpu.VMEM((8192, 128), F32),
            pltpu.VMEM((slots, 128), F32),
            pltpu.VMEM((slots, 128), F32),
        ],
        compiler_params=pltpu.CompilerParams(vmem_limit_bytes=44 * 2**20),
        name="planes",
    )(stick_pos, sticks, parity, pot, ty, ax, bx, by)


def rotate_kernel(coef_ref, image_ref, ritz_ref, base_ref, out_ref, split_ref):
    @pl.when((pl.program_id(0) == 0) & (pl.program_id(1) == 0))
    def _():
        for term in range(2):
            for j in range(0, 4096, 512):
                high, low = split(ritz_ref[term, :, j:j + 512])
                for k, piece in enumerate((high, high, low, low)):
                    split_ref[k * 128 + term * 64:k * 128 + term * 64 + 64, j:j + 512] = piece

    rows = jnp.concatenate([coef_ref[0], image_ref[0]], axis=0).T
    high, low = split(rows)
    left = jnp.concatenate([high, low, high, low], axis=1)

    @pl.loop(0, 4096 // 512)
    def _(j):
        at = pl.ds(pl.multiple_of(j * 512, 512), 512)
        out_ref[0, :, at] = (base_ref[0, :, at].astype(F32)
                             + dot(left, split_ref[:, at])).astype(BF16)


def rotate(coef, image, ritz, base):
    window, size = coef.shape[1], coef.shape[2]
    rows = 128
    data = pl.BlockSpec((1, window, rows), lambda c, g: (c, 0, g))
    slab = pl.BlockSpec((1, rows, 4096), lambda c, g: (c, g, 0))
    return pl.pallas_call(
        rotate_kernel,
        grid=(2, size // rows),
        out_shape=jax.ShapeDtypeStruct(base.shape, BF16),
        in_specs=[data, data, pl.BlockSpec((2, window, 4096), lambda c, g: (0, 0, 0)), slab],
        out_specs=slab,
        scratch_shapes=[pltpu.VMEM((512, 4096), BF16)],
        compiler_params=pltpu.CompilerParams(vmem_limit_bytes=40 * 2**20),
        name="rotate",
    )(coef, image, ritz, base)


def local(wave_coef, potential, stick_pos, stick_count, ritz_block, slab_base):
    _, bands, slots, height = wave_coef.shape
    own_count = stick_count[lax.axis_index("tg")]
    usable = (jnp.arange(slots, dtype=jnp.int32) < own_count).astype(F32)
    masked = wave_coef * usable[None, None, :, None]
    coef = lax.all_to_all(masked, "pool", split_axis=2, concat_axis=1, tiled=True)
    ritz_full = lax.all_gather(ritz_block, "pool", axis=1, tiled=True)

    cos_z, sin_z = (t.astype(np.float32) for t in np_cs(height))
    mul = functools.partial(jnp.einsum, precision=lax.Precision.HIGHEST)
    table_f = np.stack([np.stack([cos_z, sin_z]), np.stack([-sin_z, cos_z])])
    table_b = np.stack([np.stack([cos_z, -sin_z]), np.stack([sin_z, cos_z])])
    sticks = mul("pbsz,pqzn->sqbn", masked, table_f)
    planes = lax.all_to_all(sticks, "tg", split_axis=3, concat_axis=0, tiled=True)
    columns = plane_step(planes.reshape(planes.shape[0], -1), stick_pos, potential)
    returned = lax.all_to_all(columns.reshape(planes.shape), "tg", split_axis=0, concat_axis=3, tiled=True)
    applied = mul("spbz,pqzn->qbsn", returned, table_b) * usable[None, None, :, None]
    image = lax.all_to_all(applied, "pool", split_axis=2, concat_axis=1, tiled=True)
    window = coef.shape[1]
    rotated = rotate(coef.reshape(2, window, -1), image.reshape(2, window, -1), ritz_full, slab_base)
    return applied, rotated


def solution(mesh):
    in_specs = (
        P(None, "pool", "tg", None),
        P("tg", None, None),
        P(),
        P(),
        P(None, "pool", None),
        P(None, ("tg", "pool"), None),
    )
    out_specs = (P(None, "pool", "tg", None), P(None, ("tg", "pool"), None))
    return jax.shard_map(local, mesh=mesh, in_specs=in_specs, out_specs=out_specs, check_vma=False)
```

profile of v0, /device:TPU:1, one launch (start us, length us, event | category | flops | bytes accessed | tf_op | source)
XLA Modules:
  0.0 156.6 jit_solution(3102446089541868306)
XLA Ops:
  7.2 0.0 copy-start.5
  7.2 0.0 all-gather.2.cloned.1.call-start
  7.2 1.6 %copy.62 = f32[2,4,4096]{2,0,1:T(2,128)} copy(f32[2,4,4096]{2,1,0:T(4,128)} %param.16) | data formatting | bytes 262144 | tf_op args[4]
  8.9 0.0 all-gather.2.cloned.1.call-update
  8.9 1.2 dynamic_slice.3
  10.1 0.6 compare_convert_fusion
  10.8 1.4 convolution_bitcast_fusion.1
  12.2 0.3 copy.49
  12.6 1.3 reshape.38
  13.9 7.5 %all-to-all-start = ((f32[8,1,8192]{2,1,0:T(1,128)}), f32[8,1,8192]{2,1,0:T(1,128)S(1)}, u32[]{:S(2)}, u32[]{:S(2)}) async-start(f32[8,1,8192]{2,1,0:T(1,128)} %reshape.38), calls=%async_computation | async-start | bytes 524288 | tf_op jit(solution)/shard_map/all_to_all | solution.py:218
  21.3 0.0 copy-done.5
  21.4 0.1 copy.53.parity_ref
  21.5 7.2 %all-to-all-done = f32[8,1,8192]{2,1,0:T(1,128)S(1)} async-done(((f32[8,1,8192]{2,1,0:T(1,128)}), f32[8,1,8192]{2,1,0:T(1,128)S(1)}, u32[]{:S(2)}, u32[]{:S(2)}) %all-to-all-start) | async-done | bytes 262176 | tf_op jit(solution)/shard_map/all_to_all | solution.py:218
  28.7 0.5 broadcast.5
  29.3 1.3 reduce
  30.5 0.0 copy-start.1
  30.6 0.0 copy-start.2
  30.6 0.0 copy-start.3
  30.6 0.0 copy-start.4
  30.6 0.4 reshape.39
  31.0 0.1 copy.50
  31.1 0.2 copy.51
  31.3 0.1 reshape.27
  31.4 0.1 copy.52.sticks_ref
  31.5 0.0 copy-done.1
  31.5 0.4 copy-done.2
  31.9 0.1 copy-done.3
  32.0 0.1 copy-done.4
  32.1 51.8 %planes.1 = f32[512,128]{1,0:T(8,128)S(1)} custom-call(s32[512]{0:T(512)S(1)} %copy-done.5, f32[512,128]{1,0:T(8,128)S(1)} %copy.52.sticks_ref, s32[512,1]{1,0:T(8,128)S(1)} %copy.53.parity_ref, f32[16,128,128]{2,1,0:T(8,128)S(1)} %copy-done.2, bf16[768,256]{1,0:T(8,128)(2,1)S(1)} %copy-done.4, bf16[256,768]{1,0:T(8,128)(2,1)S(1)} %copy-done.3, ...), custom_call_target="tpu_custom_call" | custom-call | tf_op jit(solution)/shard_map/planes/pallas_call | solution.py:151
  84.0 0.1 copy.54
  84.1 0.0 copy-start.6
  84.1 1.1 copy.55
  85.2 2.3 %reshape.40 = f32[8,1,8192]{2,1,0:T(1,128)} reshape(f32[512,2,4,16]{3,2,1,0:T(4,128)S(1)} %copy.55) | data formatting | bytes 524288
  87.5 4.5 %all-to-all-start.1 = ((f32[8,1,8192]{2,1,0:T(1,128)}), f32[8,1,8192]{2,1,0:T(1,128)S(1)}, u32[]{:S(2)}, u32[]{:S(2)}) async-start(f32[8,1,8192]{2,1,0:T(1,128)} %reshape.40), calls=%async_computation.1 | async-start | bytes 524288 | tf_op jit(solution)/shard_map/all_to_all | solution.py:220
  92.0 0.0 copy-done.6
  92.0 0.1 broadcast_multiply_fusion
  92.0 0.9 copy.58
  92.9 6.3 %all-to-all-done.1 = f32[8,1,8192]{2,1,0:T(1,128)S(1)} async-done(((f32[8,1,8192]{2,1,0:T(1,128)}), f32[8,1,8192]{2,1,0:T(1,128)S(1)}, u32[]{:S(2)}, u32[]{:S(2)}) %all-to-all-start.1) | async-done | bytes 262176 | tf_op jit(solution)/shard_map/all_to_all | solution.py:220
  99.2 7.8 %all-to-all-start.2 = ((f32[2,4,64,128]{3,1,0,2:T(4,128)}), f32[2,4,64,128]{3,1,0,2:T(4,128)S(1)}, u32[]{:S(2)}, u32[]{:S(2)}) async-start(f32[2,4,64,128]{3,1,0,2:T(4,128)} %copy.58), calls=%async_computation.2 | async-start | bytes 524288 | tf_op jit(solution)/shard_map/all_to_all | solution.py:210
  107.0 1.2 reduce.1
  108.3 0.0 copy-start.7
  108.3 1.5 reshape.41
  109.8 1.0 copy.73
  110.8 0.0 copy-done.7
  110.8 1.0 fusion.1
  111.8 0.9 copy.60
  112.7 1.5 all-to-all-done.2
  114.2 4.3 %all-to-all-start.3 = ((f32[2,4,64,128]{3,0,1,2:T(2,128)}), f32[2,4,64,128]{3,0,1,2:T(2,128)S(1)}, u32[]{:S(2)}, u32[]{:S(2)}) async-start(f32[2,4,64,128]{3,0,1,2:T(2,128)} %copy.60), calls=%async_computation.3 | async-start | bytes 524288 | tf_op jit(solution)/shard_map/all_to_all | solution.py:222
  118.5 0.1 copy.79
  118.6 0.1 reshape.30.coef_ref
  118.7 0.7 copy.64
  119.4 6.3 %all-to-all-done.3 = f32[2,4,64,128]{3,0,1,2:T(2,128)S(1)} async-done(((f32[2,4,64,128]{3,0,1,2:T(2,128)}), f32[2,4,64,128]{3,0,1,2:T(2,128)S(1)}, u32[]{:S(2)}, u32[]{:S(2)}) %all-to-all-start.3) | async-done | bytes 262176 | tf_op jit(solution)/shard_map/all_to_all | solution.py:222
  125.7 0.1 copy.78
  125.8 0.1 reshape.31.image_ref
  125.9 0.0 all-gather.2.cloned.1.call-done
  125.9 2.8 %copy.63.ritz_ref = f32[2,64,4096]{2,1,0:T(8,128)S(1)} copy(f32[2,64,4096]{2,0,1:T(2,128)} %all-gather.2.cloned.1.call-done) | data formatting | bytes 4194304 | tf_op jit(solution)/shard_map/all_gather | solution.py:211
  128.7 0.0 copy-start
  128.8 3.4 %copy-done = bf16[2,512,4096]{2,1,0:T(8,128)(2,1)S(1)} copy-done((bf16[2,512,4096]{2,1,0:T(8,128)(2,1)S(1)}, bf16[2,512,4096]{2,1,0:T(8,128)(2,1)}, u32[]{:S(2)}) %copy-start) | copy-done | bytes 8388632
  132.1 17.6 %rotate.1 = bf16[2,512,4096]{2,1,0:T(8,128)(2,1)} custom-call(f32[2,64,512]{2,1,0:T(8,128)S(1)} %reshape.30.coef_ref, f32[2,64,512]{2,1,0:T(8,128)S(1)} %reshape.31.image_ref, f32[2,64,4096]{2,1,0:T(8,128)S(1)} %copy.63.ritz_ref, bf16[2,512,4096]{2,1,0:T(8,128)(2,1)S(1)} %copy-done), custom_call_target="tpu_custom_call" | custom-call | tf_op jit(solution)/shard_map/rotate/pallas_call | solution.py:193
  (1 shorter events, 0.0 us)
Async XLA Ops:
  7.2 14.2 %copy-start.5 = (s32[512]{0:T(512)S(1)}, s32[512]{0:T(512)}, u32[]{:S(2)}) copy-start(s32[512]{0:T(512)} %pos_ref.1) | copy-start | bytes 6148
  7.2 118.8 %all-gather.2.cloned.1.call-start = ((), (), s32[]{:S(2)}) async-start(), calls=%async_computation.4 | async-start | bytes 2228224 | tf_op jit(solution)/shard_map/all_gather | solution.py:211
  13.9 14.9 %all-to-all-start = ((f32[8,1,8192]{2,1,0:T(1,128)}), f32[8,1,8192]{2,1,0:T(1,128)S(1)}, u32[]{:S(2)}, u32[]{:S(2)}) async-start(f32[8,1,8192]{2,1,0:T(1,128)} %reshape.38), calls=%async_computation | async-start | bytes 524288 | tf_op jit(solution)/shard_map/all_to_all | solution.py:218
  30.5 1.0 copy-start.1
  30.6 1.4 copy-start.2
  30.6 1.5 copy-start.3
  30.6 1.6 %copy-start.4 = (bf16[768,256]{1,0:T(8,128)(2,1)S(1)}, bf16[768,256]{1,0:T(8,128)(2,1)}, u32[]{:S(2)}) copy-start(bf16[768,256]{1,0:T(8,128)(2,1)} %constant.25.clone.ty_ref) | copy-start | bytes 1179652
  84.1 7.8 %copy-start.6 = (f32[2,4,64,128]{3,2,1,0:T(8,128)S(1)}, f32[2,4,64,128]{3,2,1,0:T(8,128)}, u32[]{:S(2)}) copy-start(f32[2,4,64,128]{3,2,1,0:T(8,128)} %param.12) | copy-start | bytes 786436
  87.5 11.8 %all-to-all-start.1 = ((f32[8,1,8192]{2,1,0:T(1,128)}), f32[8,1,8192]{2,1,0:T(1,128)S(1)}, u32[]{:S(2)}, u32[]{:S(2)}) async-start(f32[8,1,8192]{2,1,0:T(1,128)} %reshape.40), calls=%async_computation.1 | async-start | bytes 524288 | tf_op jit(solution)/shard_map/all_to_all | solution.py:220
  99.2 14.9 %all-to-all-start.2 = ((f32[2,4,64,128]{3,1,0,2:T(4,128)}), f32[2,4,64,128]{3,1,0,2:T(4,128)S(1)}, u32[]{:S(2)}, u32[]{:S(2)}) async-start(f32[2,4,64,128]{3,1,0,2:T(4,128)} %copy.58), calls=%async_computation.2 | async-start | bytes 524288 | tf_op jit(solution)/shard_map/all_to_all | solution.py:210
  108.3 2.5 %copy-start.7 = (f32[2,2,128,128,1]{3,2,0,1,4:T(8,128)S(1)}, f32[2,2,128,128,1]{3,2,0,1,4:T(8,128)}, u32[]{:S(2)}) copy-start(f32[2,2,128,128,1]{3,2,0,1,4:T(8,128)} %constant.32) | copy-start | bytes 786436
  114.2 11.5 %all-to-all-start.3 = ((f32[2,4,64,128]{3,0,1,2:T(2,128)}), f32[2,4,64,128]{3,0,1,2:T(2,128)S(1)}, u32[]{:S(2)}, u32[]{:S(2)}) async-start(f32[2,4,64,128]{3,0,1,2:T(2,128)} %copy.60), calls=%async_computation.3 | async-start | bytes 524288 | tf_op jit(solution)/shard_map/all_to_all | solution.py:222
  128.7 3.4 %copy-start = (bf16[2,512,4096]{2,1,0:T(8,128)(2,1)S(1)}, bf16[2,512,4096]{2,1,0:T(8,128)(2,1)}, u32[]{:S(2)}) copy-start(bf16[2,512,4096]{2,1,0:T(8,128)(2,1)} %base_ref.1) | copy-start | bytes 25165828
Sparse Core Ops, SparseCore 0:
  9.7 38.9 all-gather.1
where the time goes:
time: 157 us
  Pallas kernels  69.5 us (44%)
  starting transfers between devices  24.1 us (15%)
  local copies, waits for them, and re-layouts  21.7 us (14%)
  waiting for transfers between devices  21.4 us (14%)
  between operations  14.3 us (9%)
  other arithmetic  3.24 us (2%)
  matrix products  2.44 us (2%)
    pallas_call x1, Pallas kernels, plane_step(): pl.pallas_call(plane_kernel, out_shape=jax.ShapeDtypeStruct((slots, 128),...  51.8 us
    pallas_call x1, Pallas kernels, rotate(): pl.pallas_call(rotate_kernel, grid=(2, size // rows), out_shape=jax.Shape...  17.6 us
    unnamed x22, local copies, waits for them, and re-layouts  11.8 us
    all_to_all x1, starting transfers between devices, local(): lax.all_to_all(masked, 'pool', split_axis=2, concat_axis=1, tiled=True)  7.77 us
    all_to_all x1, starting transfers between devices, local(): lax.all_to_all(sticks, 'tg', split_axis=3, concat_axis=0, tiled=True)  7.48 us
    all_to_all x1, waiting for transfers between devices, local(): lax.all_to_all(sticks, 'tg', split_axis=3, concat_axis=0, tiled=True)  7.23 us
    all_to_all x1, waiting for transfers between devices, local(): lax.all_to_all(applied, 'pool', split_axis=2, concat_axis=1, tiled=True)  6.33 us
    all_to_all x1, waiting for transfers between devices, local(): lax.all_to_all(columns.reshape(planes.shape), 'tg', split_axis=0, concat_...  6.32 us
  transfers between devices with their start and end apart: 5, of which 4 were waited for; matrix products, arithmetic and copies ran while one was open for 12% of the time, Pallas kernels for 33%

commit v1 on v0

--- a/solution.py
+++ b/solution.py
@@ -14,6 +14,7 @@
 NY = 128
 BF16 = jnp.bfloat16
 F32 = jnp.float32
+MESH = pl.DeviceIdType.MESH
 
 
 def np_split(table):
@@ -165,16 +166,21 @@
     )(stick_pos, sticks, parity, pot, ty, ax, bx, by)
 
 
-def rotate_kernel(coef_ref, image_ref, ritz_ref, base_ref, out_ref, split_ref):
-    @pl.when((pl.program_id(0) == 0) & (pl.program_id(1) == 0))
+def rotate_kernel(coef_ref, image_ref, ritz_ref, base_ref, applied_ref, out_ref, copy_ref, split_ref, rows_ref):
+    part, block = pl.program_id(0), pl.program_id(1)
+
+    @pl.when((part == 0) & (block == 0))
     def _():
+        copy_ref[...] = applied_ref[...]
         for term in range(2):
             for j in range(0, 4096, 512):
                 high, low = split(ritz_ref[term, :, j:j + 512])
                 for k, piece in enumerate((high, high, low, low)):
                     split_ref[k * 128 + term * 64:k * 128 + term * 64 + 64, j:j + 512] = piece
 
-    rows = jnp.concatenate([coef_ref[0], image_ref[0]], axis=0).T
+    rows_ref[:128, :] = coef_ref[...].reshape(128, 128)
+    rows_ref[128:, :] = image_ref[...].reshape(128, 128)
+    rows = rows_ref[pl.ds(part, 128, 2), :].T
     high, low = split(rows)
     left = jnp.concatenate([high, low, high, low], axis=1)
 
@@ -185,44 +191,175 @@
                              + dot(left, split_ref[:, at])).astype(BF16)
 
 
-def rotate(coef, image, ritz, base):
-    window, size = coef.shape[1], coef.shape[2]
-    rows = 128
-    data = pl.BlockSpec((1, window, rows), lambda c, g: (c, 0, g))
+def rotate(coef, image, ritz, base, applied):
+    window, rows = ritz.shape[1], coef.shape[3]
+    data = pl.BlockSpec((coef.shape[0], 1) + coef.shape[2:], lambda c, g: (0, g, 0, 0))
     slab = pl.BlockSpec((1, rows, 4096), lambda c, g: (c, g, 0))
+    whole = pl.BlockSpec(applied.shape, lambda c, g: (0, 0))
     return pl.pallas_call(
         rotate_kernel,
-        grid=(2, size // rows),
-        out_shape=jax.ShapeDtypeStruct(base.shape, BF16),
-        in_specs=[data, data, pl.BlockSpec((2, window, 4096), lambda c, g: (0, 0, 0)), slab],
-        out_specs=slab,
-        scratch_shapes=[pltpu.VMEM((512, 4096), BF16)],
+        grid=(2, coef.shape[1]),
+        out_shape=[jax.ShapeDtypeStruct(base.shape, BF16), jax.ShapeDtypeStruct(applied.shape, F32)],
+        in_specs=[data, data, pl.BlockSpec((2, window, 4096), lambda c, g: (0, 0, 0)), slab, whole],
+        out_specs=[slab, whole],
+        scratch_shapes=[pltpu.VMEM((512, 4096), BF16), pltpu.VMEM((256, 128), F32)],
         compiler_params=pltpu.CompilerParams(vmem_limit_bytes=40 * 2**20),
         name="rotate",
-    )(coef, image, ritz, base)
+    )(coef, image, ritz, base, applied)
+
+
+def greet(n_tg, n_pool, tg, pool):
+    barrier = pltpu.get_barrier_semaphore()
+    for step in range(1, n_tg):
+        pl.semaphore_signal(barrier, inc=1, device_id={"tg": lax.rem(tg + step, n_tg)}, device_id_type=MESH)
+    for step in range(1, n_pool):
+        pl.semaphore_signal(barrier, inc=1, device_id={"pool": lax.rem(pool + step, n_pool)}, device_id_type=MESH)
+    pl.semaphore_wait(barrier, n_tg + n_pool - 2)
+
+
+class Exchange:
+    def __init__(self, axis, size, me, source, target, send_sem, recv_sem, own_sem):
+        self.axis, self.size, self.me = axis, size, me
+        self.source, self.target = source, target
+        self.send_sem, self.recv_sem, self.own_sem = send_sem, recv_sem, own_sem
+
+    def remote(self, step):
+        peer = lax.rem(self.me + step, self.size)
+        return pltpu.make_async_remote_copy(
+            src_ref=self.source.at[peer], dst_ref=self.target.at[self.me],
+            send_sem=self.send_sem.at[peer], recv_sem=self.recv_sem.at[self.me],
+            device_id={self.axis: peer}, device_id_type=MESH)
+
+    def own(self):
+        return pltpu.make_async_copy(self.source.at[self.me], self.target.at[self.me], self.own_sem)
+
+    def start(self):
+        for step in range(1, self.size):
+            self.remote(step).start()
+        self.own().start()
+
+    def wait_recv(self):
+        self.own().wait()
+        for step in range(1, self.size):
+            peer = lax.rem(self.me + step, self.size)
+            pltpu.make_async_remote_copy(
+                src_ref=self.source.at[peer], dst_ref=self.target.at[peer],
+                send_sem=self.send_sem.at[peer], recv_sem=self.recv_sem.at[peer],
+                device_id={self.axis: peer}, device_id_type=MESH).wait_recv()
+
+    def wait_send(self):
+        for step in range(1, self.size):
+            self.remote(step).wait_send()
+
+
+def pack_rows(flat_ref, pack_ref, n_pool):
+    for k in range(n_pool):
+        for j in range(4):
+            for part in range(2):
+                rows = flat_ref[pl.ds(part * 256 + k * 4 + j, 4, 64), :]
+                pack_ref[k, j, pl.ds(part, 4, 2), :] = rows
+
+
+def spread_kernel(n_tg, n_pool, wave_ref, usable_ref, table_ref, planes_ref, coef_ref,
+                  flat_ref, sticks_ref, pack_ref, send_t, recv_t, send_p, recv_p, own_sem):
+    tg, pool = lax.axis_index("tg"), lax.axis_index("pool")
+    greet(n_tg, n_pool, tg, pool)
+    usable = jnp.broadcast_to(usable_ref[...], (64, 128))
+    rows = []
+    for band in range(4):
+        pair = [wave_ref[part, band] * usable for part in range(2)]
+        for part in range(2):
+            flat_ref[(part * 4 + band) * 64:(part * 4 + band + 1) * 64, :] = pair[part]
+        rows.append(jnp.concatenate(pair, axis=1))
+    res = dot(lanes3(jnp.concatenate(rows, axis=0)), table_ref[...])
+    for t in range(n_tg):
+        sticks_ref[t] = jnp.concatenate(
+            [res[band * 64:(band + 1) * 64, part * 128 + t * 16:part * 128 + t * 16 + 16]
+             for part in range(2) for band in range(4)], axis=1)
+    planes = Exchange("tg", n_tg, tg, sticks_ref, planes_ref, send_t, recv_t, own_sem.at[0])
+    planes.start()
+    pack_rows(flat_ref, pack_ref, n_pool)
+    coef = Exchange("pool", n_pool, pool, pack_ref, coef_ref, send_p, recv_p, own_sem.at[1])
+    coef.start()
+    planes.wait_recv()
+    coef.wait_recv()
+    planes.wait_send()
+    coef.wait_send()
+
+
+def collect_kernel(n_tg, n_pool, cols_ref, usable_ref, table_ref, applied_ref, image_ref,
+                   returned_ref, pack_ref, send_t, recv_t, send_p, recv_p, own_sem):
+    tg, pool = lax.axis_index("tg"), lax.axis_index("pool")
+    greet(n_tg, n_pool, tg, pool)
+    back = Exchange("tg", n_tg, tg, cols_ref, returned_ref, send_t, recv_t, own_sem.at[0])
+    back.start()
+    usable = jnp.broadcast_to(usable_ref[...], (64, 256))
+    back.wait_recv()
+    rows = []
+    for band in range(4):
+        rows.append(jnp.concatenate(
+            [returned_ref[t, :, part * 64 + band * 16:part * 64 + band * 16 + 16]
+             for part in range(2) for t in range(n_tg)], axis=1))
+    res = dot(lanes3(jnp.concatenate(rows, axis=0)), table_ref[...])
+    for band in range(4):
+        block = res[band * 64:(band + 1) * 64] * usable
+        for part in range(2):
+            at = (part * 4 + band) * 64
+            applied_ref[at:at + 64, :] = block[:, part * 128:(part + 1) * 128]
+    pack_rows(applied_ref, pack_ref, n_pool)
+    image = Exchange("pool", n_pool, pool, pack_ref, image_ref, send_p, recv_p, own_sem.at[1])
+    image.start()
+    image.wait_recv()
+    back.wait_send()
+    image.wait_send()
+
+
+def exchange_scratch(n_tg, n_pool):
+    dma = pltpu.SemaphoreType.DMA
+    return [dma((n_tg,)), dma((n_tg,)), dma((n_pool,)), dma((n_pool,)), dma((2,))]
+
+
+def spread(wave, usable, n_tg, n_pool):
+    vmem = pl.BlockSpec(memory_space=pltpu.VMEM)
+    return pl.pallas_call(
+        functools.partial(spread_kernel, n_tg, n_pool),
+        out_shape=[jax.ShapeDtypeStruct((n_tg, 64, 128), F32), jax.ShapeDtypeStruct((n_pool, 4, 8, 128), F32)],
+        in_specs=[vmem] * 3,
+        out_specs=[vmem] * 2,
+        scratch_shapes=[pltpu.VMEM((512, 128), F32), pltpu.VMEM((n_tg, 64, 128), F32),
+                        pltpu.VMEM((n_pool, 4, 8, 128), F32)] + exchange_scratch(n_tg, n_pool),
+        compiler_params=pltpu.CompilerParams(collective_id=0, has_side_effects=True,
+                                             vmem_limit_bytes=24 * 2**20),
+        name="spread",
+    )(wave, usable, as_rhs_rows(row_table(128, 1.0)))
+
+
+def collect(columns, usable, n_tg, n_pool):
+    vmem = pl.BlockSpec(memory_space=pltpu.VMEM)
+    return pl.pallas_call(
+        functools.partial(collect_kernel, n_tg, n_pool),
+        out_shape=[jax.ShapeDtypeStruct((512, 128), F32), jax.ShapeDtypeStruct((n_pool, 4, 8, 128), F32)],
+        in_specs=[vmem] * 3,
+        out_specs=[vmem] * 2,
+        scratch_shapes=[pltpu.VMEM((n_tg, 64, 128), F32),
+                        pltpu.VMEM((n_pool, 4, 8, 128), F32)] + exchange_scratch(n_tg, n_pool),
+        compiler_params=pltpu.CompilerParams(collective_id=1, has_side_effects=True,
+                                             vmem_limit_bytes=24 * 2**20),
+        name="collect",
+    )(columns, usable, as_rhs_rows(row_table(128, -1.0)))
 
 
 def local(wave_coef, potential, stick_pos, stick_count, ritz_block, slab_base):
-    _, bands, slots, height = wave_coef.shape
+    n_tg, n_pool = lax.axis_size("tg"), lax.axis_size("pool")
+    slots = wave_coef.shape[2]
     own_count = stick_count[lax.axis_index("tg")]
-    usable = (jnp.arange(slots, dtype=jnp.int32) < own_count).astype(F32)
-    masked = wave_coef * usable[None, None, :, None]
-    coef = lax.all_to_all(masked, "pool", split_axis=2, concat_axis=1, tiled=True)
+    usable = (jnp.arange(slots, dtype=jnp.int32) < own_count).astype(F32).reshape(slots, 1)
     ritz_full = lax.all_gather(ritz_block, "pool", axis=1, tiled=True)
-
-    cos_z, sin_z = (t.astype(np.float32) for t in np_cs(height))
-    mul = functools.partial(jnp.einsum, precision=lax.Precision.HIGHEST)
-    table_f = np.stack([np.stack([cos_z, sin_z]), np.stack([-sin_z, cos_z])])
-    table_b = np.stack([np.stack([cos_z, -sin_z]), np.stack([sin_z, cos_z])])
-    sticks = mul("pbsz,pqzn->sqbn", masked, table_f)
-    planes = lax.all_to_all(sticks, "tg", split_axis=3, concat_axis=0, tiled=True)
-    columns = plane_step(planes.reshape(planes.shape[0], -1), stick_pos, potential)
-    returned = lax.all_to_all(columns.reshape(planes.shape), "tg", split_axis=0, concat_axis=3, tiled=True)
-    applied = mul("spbz,pqzn->qbsn", returned, table_b) * usable[None, None, :, None]
-    image = lax.all_to_all(applied, "pool", split_axis=2, concat_axis=1, tiled=True)
-    window = coef.shape[1]
-    rotated = rotate(coef.reshape(2, window, -1), image.reshape(2, window, -1), ritz_full, slab_base)
-    return applied, rotated
+    planes, coef = spread(wave_coef, usable, n_tg, n_pool)
+    columns = plane_step(planes.reshape(n_tg * slots, 128), stick_pos, potential)
+    applied, image = collect(columns.reshape(n_tg, slots, 128), usable, n_tg, n_pool)
+    rotated, applied = rotate(coef, image, ritz_full, slab_base, applied)
+    return applied.reshape(wave_coef.shape), rotated
 
 
 def solution(mesh):

time: 157 us -> 137 us (0.87)
  Pallas kernels: 69.5 us -> 104 us
  starting transfers between devices: 24.1 us -> 0.04 us
  waiting for transfers between devices: 21.4 us -> 0.04 us
  local copies, waits for them, and re-layouts: 21.7 us -> 17.1 us
  matrix products: 2.44 us -> 0 us
  other arithmetic: 3.24 us -> 1.34 us
    pallas_call x1 -> x3, Pallas kernels: 17.6 us -> 52.5 us  [the longest x1 18.2 us: spread(): pl.pallas_call(functools.partial(spread_kernel, n_tg, n_pool), out_shape=...]
    all_to_all x4 -> x0, starting transfers between devices: 24 us -> none  [the longest x1 7.77 us: local(): lax.all_to_all(masked, 'pool', split_axis=2, concat_axis=1, tiled=True)]
    all_to_all x4 -> x0, waiting for transfers between devices: 21.3 us -> none  [the longest x1 7.23 us: local(): lax.all_to_all(sticks, 'tg', split_axis=3, concat_axis=0, tiled=True)]
    all_to_all x2 -> x0, other arithmetic: 2.5 us -> none  [the longest x1 1.26 us: local(): lax.all_to_all(sticks, 'tg', split_axis=3, concat_axis=0, tiled=True)]
    dot_general x2 -> x0, matrix products: 2.44 us -> none  [the longest x1 1.44 us: local(): sticks = mul('pbsz,pqzn->sqbn', masked, table_f)]
    all_to_all x6 -> x0, local copies, waits for them, and re-layouts: 1.96 us -> none  [the longest x1 1.02 us: local(): lax.all_to_all(columns.reshape(planes.shape), 'tg', split_axis=0, concat_...]
    mul x2 -> x0, local copies, waits for them, and re-layouts: 1.77 us -> none  [the longest x1 0.9 us: local(): mul('spbz,pqzn->qbsn', returned, table_b) * usable[None, None, :, None]]
    unnamed x22 -> x19, local copies, waits for them, and re-layouts: 11.8 us -> 12.9 us
  transfers between devices with their start and end apart: 5 -> 1, of which waited for: 4 -> 0; matrix products, arithmetic and copies ran while one was open for 12% -> 2% of each run, Pallas kernels for 33% -> 63%
where the time goes in v1:
time: 137 us
  Pallas kernels  104 us (76%)
  local copies, waits for them, and re-layouts  17.1 us (12%)
  between operations  14.1 us (10%)
    pallas_call x1, Pallas kernels, plane_step(): pl.pallas_call(plane_kernel, out_shape=jax.ShapeDtypeStruct((slots, 128),...  51.4 us
    pallas_call x1, Pallas kernels, spread(): pl.pallas_call(functools.partial(spread_kernel, n_tg, n_pool), out_shape=...  18.2 us
    pallas_call x1, Pallas kernels, rotate(): pl.pallas_call(rotate_kernel, grid=(2, coef.shape[1]), out_shape=[jax.Sha...  17.9 us
    pallas_call x1, Pallas kernels, collect(): pl.pallas_call(functools.partial(collect_kernel, n_tg, n_pool), out_shape...  16.4 us
    unnamed x19, local copies, waits for them, and re-layouts  12.9 us
    all_gather x1, local copies, waits for them, and re-layouts, local(): ritz_full = lax.all_gather(ritz_block, 'pool', axis=1, tiled=True)  2.81 us
  transfers between devices with their start and end apart: 1, of which 0 were waited for; matrix products, arithmetic and copies ran while one was open for 2% of the time, Pallas kernels for 63%

profile of v1, /device:TPU:1, one launch (start us, length us, event | category | flops | bytes accessed | tf_op | source)
XLA Modules:
  0.0 136.6 jit_solution(17552236530203742328)
XLA Ops:
  7.2 0.0 all-gather.2.cloned.1.call-start
  7.2 1.7 %copy.16 = f32[2,4,4096]{2,0,1:T(2,128)} copy(f32[2,4,4096]{2,1,0:T(4,128)} %param.16) | data formatting | bytes 262144 | tf_op args[4]
  8.9 0.0 all-gather.2.cloned.1.call-update
  8.9 0.7 shift-right-arithmetic_and_fusion
  9.6 0.1 copy.15.parity_ref
  9.7 1.2 dynamic_slice.3
  11.0 0.7 fusion.usable_ref
  11.6 0.0 copy-start.1
  11.7 1.0 copy-done.1
  12.6 0.0 copy-start.7
  12.6 0.9 copy-done.7
  13.6 18.2 %spread.1 = (f32[8,64,128]{2,1,0:T(8,128)S(1)}, f32[16,4,8,128]{3,2,1,0:T(8,128)S(1)}) custom-call(f32[2,4,64,128]{3,2,1,0:T(8,128)S(1)} %copy-done.7, f32[64,1]{1,0:T(8,128)S(1)} %fusion.usable_ref, bf16[768,256]{1,0:T(8,128)(2,1)S(1)} %copy-done.1), custom_call_target="tpu_custom_call" | custom-call | tf_op jit(solution)/shard_map/spread/pallas_call | solution.py:324
  31.8 0.0 copy-start.2
  31.9 1.0 copy-done.2
  32.9 0.0 copy-start.3
  32.9 1.0 copy-done.3
  33.9 0.0 copy-start.4
  33.9 1.2 copy-done.4
  35.1 0.0 copy-start.6
  35.1 1.0 copy-done.6
  36.1 0.0 copy-start.8
  36.1 0.7 copy-done.8
  36.8 51.4 %planes.1 = f32[512,128]{1,0:T(8,128)S(1)} custom-call(s32[512]{0:T(512)S(1)} %copy-done.8, f32[512,128]{1,0:T(8,128)S(1)} %bitcast.6, s32[512,1]{1,0:T(8,128)S(1)} %copy.15.parity_ref, f32[16,128,128]{2,1,0:T(8,128)S(1)} %copy-done.4, bf16[768,256]{1,0:T(8,128)(2,1)S(1)} %copy-done.2, bf16[256,768]{1,0:T(8,128)(2,1)S(1)} %copy-done.6, ...), custom_call_target="tpu_custom_call" | custom-call | tf_op jit(solution)/shard_map/planes/pallas_call | solution.py:152
  88.2 0.0 copy-start.5
  88.2 1.0 copy-done.5
  89.2 16.4 %collect.1 = (f32[512,128]{1,0:T(8,128)S(1)}, f32[16,4,8,128]{3,2,1,0:T(8,128)S(1)}) custom-call(f32[8,64,128]{2,1,0:T(8,128)S(1)} %bitcast.5, f32[64,1]{1,0:T(8,128)S(1)} %fusion.usable_ref, bf16[768,256]{1,0:T(8,128)(2,1)S(1)} %copy-done.5), custom_call_target="tpu_custom_call" | custom-call | tf_op jit(solution)/shard_map/collect/pallas_call | solution.py:339
  105.6 0.0 all-gather.2.cloned.1.call-done
  105.7 2.8 %copy.17.ritz_ref = f32[2,64,4096]{2,1,0:T(8,128)S(1)} copy(f32[2,64,4096]{2,0,1:T(2,128)} %all-gather.2.cloned.1.call-done) | data formatting | bytes 4194304 | tf_op jit(solution)/shard_map/all_gather | solution.py:357
  108.5 0.0 copy-start
  108.5 3.4 %copy-done = bf16[2,512,4096]{2,1,0:T(8,128)(2,1)S(1)} copy-done((bf16[2,512,4096]{2,1,0:T(8,128)(2,1)S(1)}, bf16[2,512,4096]{2,1,0:T(8,128)(2,1)}, u32[]{:S(2)}) %copy-start) | copy-done | bytes 8388632
  111.8 17.9 %rotate.1 = (bf16[2,512,4096]{2,1,0:T(8,128)(2,1)}, f32[512,128]{1,0:T(8,128)}) custom-call(f32[16,4,8,128]{3,2,1,0:T(8,128)S(1)} %get-tuple-element.8.coef_ref, f32[16,4,8,128]{3,2,1,0:T(8,128)S(1)} %get-tuple-element.10.image_ref, f32[2,64,4096]{2,1,0:T(8,128)S(1)} %copy.17.ritz_ref, bf16[2,512,4096]{2,1,0:T(8,128)(2,1)S(1)} %copy-done, ...), custom_call_target="tpu_custom_call" | custom-call | tf_op jit(solution)/shard_map/rotate/pallas_call | solution.py:199
Async XLA Ops:
  7.2 98.5 %all-gather.2.cloned.1.call-start = ((), (), s32[]{:S(2)}) async-start(), calls=%async_computation | async-start | bytes 2228224 | tf_op jit(solution)/shard_map/all_gather | solution.py:357
  11.6 1.0 copy-start.1
  12.6 0.9 copy-start.7
  31.8 1.0 copy-start.2
  32.9 1.0 copy-start.3
  33.9 1.2 copy-start.4
  35.1 1.0 copy-start.6
  36.1 0.7 copy-start.8
  88.2 1.0 copy-start.5
  108.5 3.4 %copy-start = (bf16[2,512,4096]{2,1,0:T(8,128)(2,1)S(1)}, bf16[2,512,4096]{2,1,0:T(8,128)(2,1)}, u32[]{:S(2)}) copy-start(bf16[2,512,4096]{2,1,0:T(8,128)(2,1)} %base_ref.1) | copy-start | bytes 25165828
Sparse Core Ops, SparseCore 0:
  10.3 40.4 all-gather.1

commit v2 on v1

v2 whole, which is shorter than its diff:
```python
import functools
import math

import jax
import jax.numpy as jnp
import ml_dtypes
import numpy as np
from jax import lax
from jax.experimental import pallas as pl
from jax.experimental.pallas import tpu as pltpu
from jax.sharding import PartitionSpec as P

NX = 128
NY = 128
BF16 = jnp.bfloat16
F32 = jnp.float32
MESH = pl.DeviceIdType.MESH


def np_split(table):
    high = table.astype(np.float32).astype(ml_dtypes.bfloat16)
    low = (table - high.astype(np.float64)).astype(ml_dtypes.bfloat16)
    return high, low


def np_cs(length):
    idx = np.arange(length)
    ang = (idx[:, None] * idx[None, :] % length) * (2.0 * math.pi / length)
    return np.cos(ang), np.sin(ang)


def row_table(length, sign, scale=1.0):
    cos_t, sin_t = np_cs(length)
    return scale * np.block([[cos_t, sign * sin_t], [-sign * sin_t, cos_t]])


def split(values):
    high = values.astype(BF16)
    low = (values - high.astype(F32)).astype(BF16)
    return high, low


def as_rhs_rows(table):
    high, low = np_split(table)
    return np.concatenate([high, high, low], axis=0)


def as_lhs(table):
    high, low = np_split(table)
    return np.concatenate([high, high, low], axis=1)


def lanes3(values):
    high, low = split(values)
    return jnp.concatenate([high, low, high], axis=1)


def rows3(values):
    high, low = split(values)
    return jnp.concatenate([high, low, high], axis=0)


def dot(a, b):
    return lax.dot_general(a, b, (((1,), (0,)), ((), ())), preferred_element_type=F32)


def dot_nt(a, b):
    return lax.dot_general(a, b, (((1,), (1,)), ((), ())), preferred_element_type=F32)


PITCH = 65
Y_STEP = 16
X_STEP = 2


def plane_kernel(pos_hbm, sticks_ref, pot_hbm, ty_hbm, ax_hbm, bx_hbm,
                 out_ref, pos_ref, pot_ref, ty_ref, ax_ref, bx_ref, grid_ref, re_ref, im_ref, sems):
    slots = sticks_ref.shape[0]
    half = 64
    pairs = [(pos_hbm, pos_ref), (ty_hbm, ty_ref), (ax_hbm, ax_ref), (bx_hbm, bx_ref), (pot_hbm, pot_ref)]
    copies = [pltpu.make_async_copy(src, dst, sems.at[k]) for k, (src, dst) in enumerate(pairs)]
    for copy in copies:
        copy.start()

    @pl.loop(0, 32)
    def _(x):
        grid_ref[pl.ds(pl.multiple_of(x * 512, 512), 512), :] = jnp.zeros((512, 128), F32)

    copies[0].wait()

    @pl.loop(0, slots // 8)
    def _(block):
        base = pl.multiple_of(block * 8, 8)
        rows = sticks_ref[pl.ds(base, 8), :]
        for k in range(8):
            grid_ref[pl.ds(pos_ref[base + k], 1), :] = rows[k:k + 1, :]

    copies[1].wait()

    @pl.loop(0, 128 // Y_STEP)
    def _(step):
        parts = []
        for k in range(Y_STEP):
            x = step * Y_STEP + k
            flipped = grid_ref[pl.ds(pl.multiple_of(x * 128, 128), 128), :].T
            parts.append(jnp.concatenate([flipped[:half], flipped[half:]], axis=1))
        res = dot(lanes3(jnp.concatenate(parts, axis=0)), ty_ref[...])
        for k in range(Y_STEP):
            to = pl.ds((step * Y_STEP + k) * PITCH, half)
            re_ref[to, :] = res[k * half:(k + 1) * half, :128]
            im_ref[to, :] = res[k * half:(k + 1) * half, 128:]

    for copy in copies[2:]:
        copy.wait()

    @pl.loop(0, 16, unroll=2)
    def _(z):
        pot = pot_ref[z]
        wide = jnp.concatenate([pot] * X_STEP, axis=1)
        wide = jnp.concatenate([wide, wide], axis=0)
        for group in range(4 // X_STEP):
            at = [pl.ds((group * X_STEP + k) * 16 + z, 128, PITCH) for k in range(X_STEP)]
            data = jnp.concatenate(
                [jnp.concatenate([re_ref[a, :], im_ref[a, :]], axis=0) for a in at], axis=1)
            field = dot(ax_ref[...], rows3(data))
            back = dot(bx_ref[...], rows3(field * wide))
            for k in range(X_STEP):
                re_ref[at[k], :] = back[:128, k * 128:(k + 1) * 128]
                im_ref[at[k], :] = back[128:, k * 128:(k + 1) * 128]

    @pl.loop(0, 128 // Y_STEP)
    def _(step):
        data = jnp.concatenate(
            [jnp.concatenate([ref[pl.ds((step * Y_STEP + k) * PITCH, half), :] for k in range(Y_STEP)], axis=0)
             for ref in (re_ref, im_ref)], axis=1)
        res = dot_nt(bx_ref[...], lanes3(data))
        for k in range(Y_STEP):
            to = pl.ds(pl.multiple_of((step * Y_STEP + k) * 128, 128), 128)
            grid_ref[to, :] = jnp.concatenate(
                [res[:128, k * half:(k + 1) * half], res[128:, k * half:(k + 1) * half]], axis=1)

    @pl.loop(0, slots // 8)
    def _(block):
        base = pl.multiple_of(block * 8, 8)
        out_ref[pl.ds(base, 8), :] = jnp.concatenate(
            [grid_ref[pl.ds(pos_ref[base + k], 1), :] for k in range(8)], axis=0)


def plane_step(sticks, stick_pos, pot):
    slots = sticks.shape[0]
    volume = 128.0 ** 3
    ty = as_rhs_rows(row_table(128, 1.0))
    ax = as_lhs(row_table(128, 1.0, 1.0 / volume).T)
    bx = as_lhs(row_table(128, -1.0).T)
    vmem = pl.BlockSpec(memory_space=pltpu.VMEM)
    hbm = pl.BlockSpec(memory_space=pltpu.HBM)
    return pl.pallas_call(
        plane_kernel,
        out_shape=jax.ShapeDtypeStruct((slots, 128), F32),
        in_specs=[hbm, vmem] + [hbm] * 4,
        out_specs=vmem,
        scratch_shapes=[
            pltpu.SMEM((slots,), jnp.int32),
            pltpu.VMEM((16, 128, 128), F32),
            pltpu.VMEM((768, 256), BF16),
            pltpu.VMEM((256, 768), BF16),
            pltpu.VMEM((256, 768), BF16),
            pltpu.VMEM((16384, 128), F32),
            pltpu.VMEM((128 * PITCH, 128), F32),
            pltpu.VMEM((128 * PITCH, 128), F32),
            pltpu.SemaphoreType.DMA((5,)),
        ],
        compiler_params=pltpu.CompilerParams(vmem_limit_bytes=52 * 2**20),
        name="planes",
    )(stick_pos, sticks, pot, ty, ax, bx)


COLUMNS = 512


def rotate_kernel(coef_ref, image_ref, applied_ref, ritz_ref, base_ref, out_ref, copy_ref, left_ref):
    @pl.when(pl.program_id(0) == 0)
    def _():
        copy_ref[...] = applied_ref[...]
        for part in range(2):
            for slot in range(4):
                rows = jnp.concatenate(
                    [ref[k, slot, part * 4:part * 4 + 4, :] for k in range(16) for ref in (coef_ref, image_ref)],
                    axis=0).T
                high, low = split(rows)
                at = (part * 4 + slot) * 128
                left_ref[at:at + 128, :] = jnp.concatenate([high, low, high, low], axis=1)

    high, low = split(ritz_ref[...])
    right = jnp.concatenate([high, high, low, low], axis=0)
    for part in range(2):
        out_ref[part] = (base_ref[part].astype(F32)
                         + dot(left_ref[part * 512:(part + 1) * 512, :], right)).astype(BF16)


def rotate(coef, image, ritz, base, applied):
    once = lambda a: pl.BlockSpec(a.shape, lambda j: (0,) * a.ndim)
    slab = pl.BlockSpec((2, base.shape[1], COLUMNS), lambda j: (0, 0, j))
    return pl.pallas_call(
        rotate_kernel,
        grid=(base.shape[2] // COLUMNS,),
        out_shape=[jax.ShapeDtypeStruct(base.shape, BF16), jax.ShapeDtypeStruct(applied.shape, F32)],
        in_specs=[once(coef), once(image), once(applied),
                  pl.BlockSpec((ritz.shape[0], COLUMNS), lambda j: (0, j)), slab],
        out_specs=[slab, once(applied)],
        scratch_shapes=[pltpu.VMEM((1024, 512), BF16)],
        compiler_params=pltpu.CompilerParams(vmem_limit_bytes=56 * 2**20),
        name="rotate",
    )(coef, image, applied, ritz, base)


def greet(n_tg, n_pool, tg, pool):
    barrier = pltpu.get_barrier_semaphore()
    for step in range(1, n_tg):
        pl.semaphore_signal(barrier, inc=1, device_id={"tg": lax.rem(tg + step, n_tg)}, device_id_type=MESH)
    for step in range(1, n_pool):
        pl.semaphore_signal(barrier, inc=1, device_id={"pool": lax.rem(pool + step, n_pool)}, device_id_type=MESH)
    pl.semaphore_wait(barrier, n_tg + n_pool - 2)


class Exchange:
    def __init__(self, axis, size, me, source, target, send_sem, recv_sem, own_sem):
        self.axis, self.size, self.me = axis, size, me
        self.source, self.target = source, target
        self.send_sem, self.recv_sem, self.own_sem = send_sem, recv_sem, own_sem

    def remote(self, step):
        peer = lax.rem(self.me + step, self.size)
        return pltpu.make_async_remote_copy(
            src_ref=self.source.at[peer], dst_ref=self.target.at[self.me],
            send_sem=self.send_sem.at[peer], recv_sem=self.recv_sem.at[self.me],
            device_id={self.axis: peer}, device_id_type=MESH)

    def own(self):
        return pltpu.make_async_copy(self.source.at[self.me], self.target.at[self.me], self.own_sem)

    def start(self):
        for step in range(1, self.size):
            self.remote(step).start()
        self.own().start()

    def wait_recv(self):
        self.own().wait()
        for step in range(1, self.size):
            peer = lax.rem(self.me + step, self.size)
            pltpu.make_async_remote_copy(
                src_ref=self.source.at[peer], dst_ref=self.target.at[peer],
                send_sem=self.send_sem.at[peer], recv_sem=self.recv_sem.at[peer],
                device_id={self.axis: peer}, device_id_type=MESH).wait_recv()

    def wait_send(self):
        for step in range(1, self.size):
            self.remote(step).wait_send()


def pack_rows(flat_ref, pack_ref, n_pool):
    for k in range(n_pool):
        for j in range(4):
            pack_ref[k, j] = flat_ref[pl.ds(k * 4 + j, 8, 64), :]


def spread_kernel(n_tg, n_pool, wave_hbm, count_hbm, table_hbm, ritz_hbm,
                  planes_ref, coef_ref, usable_ref, ritz_ref,
                  wave_ref, count_ref, table_ref, rows_ref, flat_ref, sticks_ref, pack_ref,
                  send_t, recv_t, send_p, recv_p, own_sem, load_sem):
    tg, pool = lax.axis_index("tg"), lax.axis_index("pool")
    pairs = [(count_hbm, count_ref), (wave_hbm, wave_ref), (table_hbm, table_ref), (ritz_hbm, rows_ref)]
    loads = [pltpu.make_async_copy(src, dst, load_sem.at[k]) for k, (src, dst) in enumerate(pairs)]
    for load in loads:
        load.start()
    greet(n_tg, n_pool, tg, pool)
    for load in loads:
        load.wait()
    slot = lax.broadcasted_iota(jnp.int32, (64, 128), 0)
    usable = jnp.where(slot < count_ref[tg], 1.0, 0.0).astype(F32)
    usable_ref[...] = usable
    rows = []
    for band in range(4):
        pair = [wave_ref[part, band] * usable for part in range(2)]
        for part in range(2):
            flat_ref[(part * 4 + band) * 64:(part * 4 + band + 1) * 64, :] = pair[part]
        rows.append(jnp.concatenate(pair, axis=1))
    res = dot(lanes3(jnp.concatenate(rows, axis=0)), table_ref[...])
    for t in range(n_tg):
        sticks_ref[t] = jnp.concatenate(
            [res[band * 64:(band + 1) * 64, part * 128 + t * 16:part * 128 + t * 16 + 16]
             for part in range(2) for band in range(4)], axis=1)
    planes = Exchange("tg", n_tg, tg, sticks_ref, planes_ref, send_t, recv_t, own_sem.at[0])
    planes.start()
    pack_rows(flat_ref, pack_ref, n_pool)
    coef = Exchange("pool", n_pool, pool, pack_ref, coef_ref, send_p, recv_p, own_sem.at[1])
    coef.start()
    for term in range(2):
        ritz_ref[term * 4:term * 4 + 4, :] = rows_ref[term]
    planes.wait_recv()
    coef.wait_recv()
    planes.wait_send()
    coef.wait_send()


def collect_kernel(n_tg, n_pool, cols_ref, usable_ref, table_hbm, applied_ref, image_ref,
                   table_ref, returned_ref, pack_ref, send_t, recv_t, send_p, recv_p, own_sem, load_sem):
    tg, pool = lax.axis_index("tg"), lax.axis_index("pool")
    load = pltpu.make_async_copy(table_hbm, table_ref, load_sem.at[0])
    load.start()
    greet(n_tg, n_pool, tg, pool)
    back = Exchange("tg", n_tg, tg, cols_ref, returned_ref, send_t, recv_t, own_sem.at[0])
    back.start()
    usable = usable_ref[...]
    load.wait()
    back.wait_recv()
    rows = []
    for band in range(4):
        rows.append(jnp.concatenate(
            [returned_ref[t, :, part * 64 + band * 16:part * 64 + band * 16 + 16]
             for part in range(2) for t in range(n_tg)], axis=1))
    res = dot(lanes3(jnp.concatenate(rows, axis=0)), table_ref[...])
    for band in range(4):
        for part in range(2):
            at = (part * 4 + band) * 64
            applied_ref[at:at + 64, :] = res[band * 64:(band + 1) * 64, part * 128:(part + 1) * 128] * usable
    pack_rows(applied_ref, pack_ref, n_pool)
    image = Exchange("pool", n_pool, pool, pack_ref, image_ref, send_p, recv_p, own_sem.at[1])
    image.start()
    image.wait_recv()
    back.wait_send()
    image.wait_send()


def exchange_scratch(n_tg, n_pool):
    dma = pltpu.SemaphoreType.DMA
    return [dma((n_tg,)), dma((n_tg,)), dma((n_pool,)), dma((n_pool,)), dma((2,))]


def spread(wave, count, ritz, n_tg, n_pool):
    vmem = pl.BlockSpec(memory_space=pltpu.VMEM)
    hbm = pl.BlockSpec(memory_space=pltpu.HBM)
    return pl.pallas_call(
        functools.partial(spread_kernel, n_tg, n_pool),
        out_shape=[jax.ShapeDtypeStruct((n_tg, 64, 128), F32), jax.ShapeDtypeStruct((n_pool, 4, 8, 128), F32),
                   jax.ShapeDtypeStruct((64, 128), F32), jax.ShapeDtypeStruct((8, ritz.shape[2]), F32)],
        in_specs=[hbm] * 4,
        out_specs=[vmem] * 4,
        scratch_shapes=[pltpu.VMEM(wave.shape, F32), pltpu.SMEM(count.shape, jnp.int32),
                        pltpu.VMEM((768, 256), BF16), pltpu.VMEM(ritz.shape, F32),
                        pltpu.VMEM((512, 128), F32), pltpu.VMEM((n_tg, 64, 128), F32),
                        pltpu.VMEM((n_pool, 4, 8, 128), F32)] + exchange_scratch(n_tg, n_pool)
        + [pltpu.SemaphoreType.DMA((4,))],
        compiler_params=pltpu.CompilerParams(collective_id=0, has_side_effects=True,
                                             vmem_limit_bytes=48 * 2**20),
        name="spread",
    )(wave, count, as_rhs_rows(row_table(128, 1.0)), ritz)


def collect(columns, usable, n_tg, n_pool):
    vmem = pl.BlockSpec(memory_space=pltpu.VMEM)
    hbm = pl.BlockSpec(memory_space=pltpu.HBM)
    return pl.pallas_call(
        functools.partial(collect_kernel, n_tg, n_pool),
        out_shape=[jax.ShapeDtypeStruct((512, 128), F32), jax.ShapeDtypeStruct((n_pool, 4, 8, 128), F32)],
        in_specs=[vmem, vmem, hbm],
        out_specs=[vmem] * 2,
        scratch_shapes=[pltpu.VMEM((768, 256), BF16), pltpu.VMEM((n_tg, 64, 128), F32),
                        pltpu.VMEM((n_pool, 4, 8, 128), F32)] + exchange_scratch(n_tg, n_pool)
        + [pltpu.SemaphoreType.DMA((1,))],
        compiler_params=pltpu.CompilerParams(collective_id=1, has_side_effects=True,
                                             vmem_limit_bytes=48 * 2**20),
        name="collect",
    )(columns, usable, as_rhs_rows(row_table(128, -1.0)))


def local(wave_coef, potential, stick_pos, stick_count, ritz_block, slab_base):
    n_tg, n_pool = lax.axis_size("tg"), lax.axis_size("pool")
    slots = wave_coef.shape[2]
    planes, coef, usable, ritz_rows = spread(wave_coef, stick_count, ritz_block, n_tg, n_pool)
    ritz_full = lax.all_gather(ritz_rows, "pool", axis=0, tiled=True)
    columns = plane_step(planes.reshape(n_tg * slots, 128), stick_pos, potential)
    applied, image = collect(columns.reshape(n_tg, slots, 128), usable, n_tg, n_pool)
    rotated, applied = rotate(coef, image, ritz_full, slab_base, applied)
    return applied.reshape(wave_coef.shape), rotated


def solution(mesh):
    in_specs = (
        P(None, "pool", "tg", None),
        P("tg", None, None),
        P(),
        P(),
        P(None, "pool", None),
        P(None, ("tg", "pool"), None),
    )
    out_specs = (P(None, "pool", "tg", None), P(None, ("tg", "pool"), None))
    return jax.shard_map(local, mesh=mesh, in_specs=in_specs, out_specs=out_specs, check_vma=False)
```

time: 137 us -> 94.9 us (0.69)
  Pallas kernels: 104 us -> 69.9 us
  local copies, waits for them, and re-layouts: 17.1 us -> 10.3 us
    pallas_call x1, Pallas kernels: 51.4 us -> 24.1 us  [plane_step(): pl.pallas_call(plane_kernel, out_shape=jax.ShapeDtypeStruct((slots, 128),...]
    pallas_call x1, Pallas kernels: 17.9 us -> 11.7 us  [rotate(): pl.pallas_call(rotate_kernel, grid=(base.shape[2] // COLUMNS,), out_shape...]
    all_gather x1 -> x0, local copies, waits for them, and re-layouts: 2.81 us -> none  [local(): ritz_full = lax.all_gather(ritz_block, 'pool', axis=1, tiled=True)]
    unnamed x19 -> x24, local copies, waits for them, and re-layouts: 12.9 us -> 10.3 us
  transfers between devices with their start and end apart: 1 -> 1, of which waited for: 0 -> 0; matrix products, arithmetic and copies ran while one was open for 2% -> 0% of each run, Pallas kernels for 63% -> 43%
where the time goes in v2:
time: 94.9 us; the launch traced here: 94.3 us
  Pallas kernels  69.9 us (74%)
  between operations  14.1 us (15%)
  local copies, waits for them, and re-layouts  10.3 us (11%)
    pallas_call x1, Pallas kernels, plane_step(): pl.pallas_call(plane_kernel, out_shape=jax.ShapeDtypeStruct((slots, 128),...  24.1 us
    pallas_call x1, Pallas kernels, spread(): pl.pallas_call(functools.partial(spread_kernel, n_tg, n_pool), out_shape=...  17.9 us
    pallas_call x1, Pallas kernels, collect(): pl.pallas_call(functools.partial(collect_kernel, n_tg, n_pool), out_shape...  16.2 us
    pallas_call x1, Pallas kernels, rotate(): pl.pallas_call(rotate_kernel, grid=(base.shape[2] // COLUMNS,), out_shape...  11.7 us
    unnamed x24, local copies, waits for them, and re-layouts  10.3 us
  transfers between devices with their start and end apart: 1, of which 0 were waited for; matrix products, arithmetic and copies ran while one was open for 0% of the time, Pallas kernels for 43%

profile of v2, /device:TPU:1, one launch (start us, length us, event | category | flops | bytes accessed | tf_op | source)
XLA Modules:
  0.0 94.3 jit_solution(12695502401506627487)
XLA Ops:
  7.2 0.0 all-gather.2.cloned.1.call-start
  7.2 0.0 copy-start
  7.2 1.0 %copy-done = bf16[768,256]{1,0:T(8,128)(2,1)S(1)} copy-done((bf16[768,256]{1,0:T(8,128)(2,1)S(1)}, bf16[768,256]{1,0:T(8,128)(2,1)}, u32[]{:S(2)}) %copy-start) | copy-done | bytes 393240
  8.2 0.0 copy-start.8
  8.2 0.9 %copy-done.8 = f32[2,4,64,128]{3,2,1,0:T(8,128)S(1)} copy-done((f32[2,4,64,128]{3,2,1,0:T(8,128)S(1)}, f32[2,4,64,128]{3,2,1,0:T(8,128)}, u32[]{:S(2)}) %copy-start.8) | copy-done | bytes 262168
  9.2 0.0 copy-start.9
  9.2 0.9 copy-done.9
  10.1 0.0 copy-start.11
  10.1 0.7 copy-done.11
  10.7 17.9 %spread.1 = (f32[8,64,128]{2,1,0:T(8,128)S(1)}, f32[16,4,8,128]{3,2,1,0:T(8,128)S(1)}, f32[64,128]{1,0:T(8,128)S(1)}, f32[8,4096]{1,0:T(8,128)}) custom-call(f32[2,4,64,128]{3,2,1,0:T(8,128)S(1)} %copy-done.8, s32[8]{0:T(128)S(1)} %copy-done.11, bf16[768,256]{1,0:T(8,128)(2,1)S(1)} %copy-done, f32[2,4,4096]{2,1,0:T(4,128)S(1)} %copy-done.9), custom_call_target="tpu_custom_call" | custom-call | tf_op jit(solution)/shard_map/spread/pallas_call | solution.py:343
  28.6 0.0 copy-start.5
  28.6 0.7 copy-done.5
  29.3 0.0 all-gather.2.cloned.1.call-update
  29.4 0.0 copy-start.1
  29.4 1.0 %copy-done.1 = bf16[768,256]{1,0:T(8,128)(2,1)S(1)} copy-done((bf16[768,256]{1,0:T(8,128)(2,1)S(1)}, bf16[768,256]{1,0:T(8,128)(2,1)}, u32[]{:S(2)}) %copy-start.1) | copy-done | bytes 393240
  30.4 0.0 copy-start.2
  30.4 1.0 %copy-done.2 = bf16[256,768]{1,0:T(8,128)(2,1)S(1)} copy-done((bf16[256,768]{1,0:T(8,128)(2,1)S(1)}, bf16[256,768]{1,0:T(8,128)(2,1)}, u32[]{:S(2)}) %copy-start.2) | copy-done | bytes 393240
  31.4 0.0 copy-start.3
  31.4 1.0 %copy-done.3 = bf16[256,768]{1,0:T(8,128)(2,1)S(1)} copy-done((bf16[256,768]{1,0:T(8,128)(2,1)S(1)}, bf16[256,768]{1,0:T(8,128)(2,1)}, u32[]{:S(2)}) %copy-start.3) | copy-done | bytes 393240
  32.4 0.0 copy-start.10
  32.4 0.7 copy-done.10
  33.0 24.1 %planes.1 = f32[512,128]{1,0:T(8,128)S(1)} custom-call(s32[512]{0:T(512)S(1)} %copy-done.10, f32[512,128]{1,0:T(8,128)S(1)} %bitcast.4, f32[16,128,128]{2,1,0:T(8,128)} %pot_hbm.1, bf16[768,256]{1,0:T(8,128)(2,1)S(1)} %copy-done.1, bf16[256,768]{1,0:T(8,128)(2,1)S(1)} %copy-done.3, bf16[256,768]{1,0:T(8,128)(2,1)S(1)} %copy-done.2), custom_call_target="tpu_custom_call" | custom-call | tf_op jit(solution)/shard_map/planes/pallas_call | solution.py:157
  57.1 0.0 copy-start.4
  57.1 1.0 %copy-done.4 = bf16[768,256]{1,0:T(8,128)(2,1)S(1)} copy-done((bf16[768,256]{1,0:T(8,128)(2,1)S(1)}, bf16[768,256]{1,0:T(8,128)(2,1)}, u32[]{:S(2)}) %copy-start.4) | copy-done | bytes 393240
  58.1 16.2 %collect.1 = (f32[512,128]{1,0:T(8,128)S(1)}, f32[16,4,8,128]{3,2,1,0:T(8,128)S(1)}) custom-call(f32[8,64,128]{2,1,0:T(8,128)S(1)} %bitcast.3, f32[64,128]{1,0:T(8,128)S(1)} %get-tuple-element.12.usable_ref, bf16[768,256]{1,0:T(8,128)(2,1)S(1)} %copy-done.4), custom_call_target="tpu_custom_call" | custom-call | tf_op jit(solution)/shard_map/collect/pallas_call | solution.py:363
  74.3 0.0 copy-start.6
  74.3 0.7 copy-done.6
  75.0 0.0 copy-start.7
  75.0 0.7 copy-done.7
  75.7 0.0 all-gather.2.cloned.1.call-done.ritz_ref
  75.7 11.7 %rotate.1 = (bf16[2,512,4096]{2,1,0:T(8,128)(2,1)}, f32[512,128]{1,0:T(8,128)}) custom-call(f32[16,4,8,128]{3,2,1,0:T(8,128)} %copy-done.5, f32[16,4,8,128]{3,2,1,0:T(8,128)} %copy-done.7, f32[512,128]{1,0:T(8,128)} %copy-done.6, f32[128,4096]{1,0:T(8,128)} %all-gather.2.cloned.1.call-done.ritz_ref, bf16[2,512,4096]{2,1,0:T(8,128)(2,1)} %base_ref.1), custom_call_target="tpu_custom_call" | custom-call | tf_op jit(solution)/shard_map/rotate/pallas_call | solution.py:204
Async XLA Ops:
  7.2 68.6 %all-gather.2.cloned.1.call-start = ((), (), s32[]{:S(2)}) async-start(), calls=%async_computation | async-start | bytes 2228224 | tf_op jit(solution)/shard_map/all_gather | solution.py:381
  7.2 1.0 %copy-start = (bf16[768,256]{1,0:T(8,128)(2,1)S(1)}, bf16[768,256]{1,0:T(8,128)(2,1)}, u32[]{:S(2)}) copy-start(bf16[768,256]{1,0:T(8,128)(2,1)} %constant.8.clone.table_hbm.ty_hbm) | copy-start | bytes 1179652
  8.2 0.9 %copy-start.8 = (f32[2,4,64,128]{3,2,1,0:T(8,128)S(1)}, f32[2,4,64,128]{3,2,1,0:T(8,128)}, u32[]{:S(2)}) copy-start(f32[2,4,64,128]{3,2,1,0:T(8,128)} %wave_hbm.1) | copy-start | bytes 786436
  9.2 0.9 copy-start.9
  10.1 0.7 copy-start.11
  28.6 0.7 copy-start.5
  29.4 1.0 %copy-start.1 = (bf16[768,256]{1,0:T(8,128)(2,1)S(1)}, bf16[768,256]{1,0:T(8,128)(2,1)}, u32[]{:S(2)}) copy-start(bf16[768,256]{1,0:T(8,128)(2,1)} %constant.8.clone.table_hbm.ty_hbm) | copy-start | bytes 1179652
  30.4 1.0 %copy-start.2 = (bf16[256,768]{1,0:T(8,128)(2,1)S(1)}, bf16[256,768]{1,0:T(8,128)(2,1)}, u32[]{:S(2)}) copy-start(bf16[256,768]{1,0:T(8,128)(2,1)} %constant.10.clone.bx_hbm) | copy-start | bytes 1179652
  31.4 1.0 %copy-start.3 = (bf16[256,768]{1,0:T(8,128)(2,1)S(1)}, bf16[256,768]{1,0:T(8,128)(2,1)}, u32[]{:S(2)}) copy-start(bf16[256,768]{1,0:T(8,128)(2,1)} %constant.9.clone.ax_hbm) | copy-start | bytes 1179652
  32.4 0.7 copy-start.10
  57.1 1.0 %copy-start.4 = (bf16[768,256]{1,0:T(8,128)(2,1)S(1)}, bf16[768,256]{1,0:T(8,128)(2,1)}, u32[]{:S(2)}) copy-start(bf16[768,256]{1,0:T(8,128)(2,1)} %constant.11.clone.table_hbm) | copy-start | bytes 1179652
  74.3 0.7 copy-start.6
  75.0 0.7 copy-start.7
Sparse Core Ops, SparseCore 0:
  29.5 33.5 all-gather.1

commit v3 on v2

--- a/solution.py
+++ b/solution.py
@@ -3,8 +3,6 @@
 
 import jax
 import jax.numpy as jnp
-import ml_dtypes
-import numpy as np
 from jax import lax
 from jax.experimental import pallas as pl
 from jax.experimental.pallas import tpu as pltpu
@@ -17,21 +15,21 @@
 MESH = pl.DeviceIdType.MESH
 
 
-def np_split(table):
-    high = table.astype(np.float32).astype(ml_dtypes.bfloat16)
-    low = (table - high.astype(np.float64)).astype(ml_dtypes.bfloat16)
-    return high, low
-
-
-def np_cs(length):
-    idx = np.arange(length)
-    ang = (idx[:, None] * idx[None, :] % length) * (2.0 * math.pi / length)
-    return np.cos(ang), np.sin(ang)
-
-
-def row_table(length, sign, scale=1.0):
-    cos_t, sin_t = np_cs(length)
-    return scale * np.block([[cos_t, sign * sin_t], [-sign * sin_t, cos_t]])
+def cos_sin():
+    row = lax.broadcasted_iota(jnp.int32, (128, 128), 0)
+    col = lax.broadcasted_iota(jnp.int32, (128, 128), 1)
+    angle = ((row * col) & 127).astype(F32) * (2.0 * math.pi / 128)
+    return split(jnp.cos(angle)) + split(jnp.sin(angle))
+
+
+def row_table(cos_t, sin_t, sign):
+    plus = sin_t if sign > 0 else -sin_t
+    return jnp.concatenate([jnp.concatenate([cos_t, plus], axis=1),
+                            jnp.concatenate([-plus, cos_t], axis=1)], axis=0)
+
+
+def table_pieces(cs, sign):
+    return row_table(cs[0], cs[2], sign), row_table(cs[1], cs[3], sign)
 
 
 def split(values):
@@ -40,14 +38,14 @@
     return high, low
 
 
-def as_rhs_rows(table):
-    high, low = np_split(table)
-    return np.concatenate([high, high, low], axis=0)
-
-
-def as_lhs(table):
-    high, low = np_split(table)
-    return np.concatenate([high, high, low], axis=1)
+def as_rhs_rows(cs, sign):
+    high, low = table_pieces(cs, sign)
+    return jnp.concatenate([high, high, low], axis=0)
+
+
+def as_lhs(cs, sign):
+    high, low = table_pieces(cs, -sign)
+    return jnp.concatenate([high, high, low], axis=1)
 
 
 def lanes3(values):
@@ -69,15 +67,17 @@
 
 
 PITCH = 65
+LIMIT = 60 * 2**20
 Y_STEP = 16
 X_STEP = 2
 
 
-def plane_kernel(pos_hbm, sticks_ref, pot_hbm, ty_hbm, ax_hbm, bx_hbm,
-                 out_ref, pos_ref, pot_ref, ty_ref, ax_ref, bx_ref, grid_ref, re_ref, im_ref, sems):
+def plane_kernel(pos_hbm, sticks_hbm, cs_hbm, pot_hbm,
+                 out_ref, pos_ref, sticks_ref, cs_ref, pot_ref, ty_ref, ax_ref, bx_ref,
+                 grid_ref, re_ref, im_ref, sems):
     slots = sticks_ref.shape[0]
     half = 64
-    pairs = [(pos_hbm, pos_ref), (ty_hbm, ty_ref), (ax_hbm, ax_ref), (bx_hbm, bx_ref), (pot_hbm, pot_ref)]
+    pairs = [(pos_hbm, pos_ref), (sticks_hbm, sticks_ref), (cs_hbm, cs_ref), (pot_hbm, pot_ref)]
     copies = [pltpu.make_async_copy(src, dst, sems.at[k]) for k, (src, dst) in enumerate(pairs)]
     for copy in copies:
         copy.start()
@@ -86,7 +86,13 @@
     def _(x):
         grid_ref[pl.ds(pl.multiple_of(x * 512, 512), 512), :] = jnp.zeros((512, 128), F32)
 
+    copies[2].wait()
+    cs = [cs_ref[k] for k in range(4)]
+    ty_ref[...] = as_rhs_rows(cs, 1)
+    ax_ref[...] = as_lhs(cs, 1) * (1.0 / 128.0 ** 3)
+    bx_ref[...] = as_lhs(cs, -1)
     copies[0].wait()
+    copies[1].wait()
 
     @pl.loop(0, slots // 8)
     def _(block):
@@ -94,8 +100,6 @@
         rows = sticks_ref[pl.ds(base, 8), :]
         for k in range(8):
             grid_ref[pl.ds(pos_ref[base + k], 1), :] = rows[k:k + 1, :]
-
-    copies[1].wait()
 
     @pl.loop(0, 128 // Y_STEP)
     def _(step):
@@ -110,8 +114,7 @@
             re_ref[to, :] = res[k * half:(k + 1) * half, :128]
             im_ref[to, :] = res[k * half:(k + 1) * half, 128:]
 
-    for copy in copies[2:]:
-        copy.wait()
+    copies[3].wait()
 
     @pl.loop(0, 16, unroll=2)
     def _(z):
@@ -146,21 +149,18 @@
             [grid_ref[pl.ds(pos_ref[base + k], 1), :] for k in range(8)], axis=0)
 
 
-def plane_step(sticks, stick_pos, pot):
+def plane_step(sticks, stick_pos, cs, pot):
     slots = sticks.shape[0]
-    volume = 128.0 ** 3
-    ty = as_rhs_rows(row_table(128, 1.0))
-    ax = as_lhs(row_table(128, 1.0, 1.0 / volume).T)
-    bx = as_lhs(row_table(128, -1.0).T)
-    vmem = pl.BlockSpec(memory_space=pltpu.VMEM)
     hbm = pl.BlockSpec(memory_space=pltpu.HBM)
     return pl.pallas_call(
         plane_kernel,
         out_shape=jax.ShapeDtypeStruct((slots, 128), F32),
-        in_specs=[hbm, vmem] + [hbm] * 4,
-        out_specs=vmem,
+        in_specs=[hbm] * 4,
+        out_specs=pl.BlockSpec(memory_space=pltpu.VMEM),
         scratch_shapes=[
             pltpu.SMEM((slots,), jnp.int32),
+            pltpu.VMEM(sticks.shape, F32),
+            pltpu.VMEM(cs.shape, BF16),
             pltpu.VMEM((16, 128, 128), F32),
             pltpu.VMEM((768, 256), BF16),
             pltpu.VMEM((256, 768), BF16),
@@ -168,11 +168,11 @@
             pltpu.VMEM((16384, 128), F32),
             pltpu.VMEM((128 * PITCH, 128), F32),
             pltpu.VMEM((128 * PITCH, 128), F32),
-            pltpu.SemaphoreType.DMA((5,)),
+            pltpu.SemaphoreType.DMA((4,)),
         ],
-        compiler_params=pltpu.CompilerParams(vmem_limit_bytes=52 * 2**20),
+        compiler_params=pltpu.CompilerParams(vmem_limit_bytes=LIMIT),
         name="planes",
-    )(stick_pos, sticks, pot, ty, ax, bx)
+    )(stick_pos, sticks, cs, pot)
 
 
 COLUMNS = 512
@@ -191,7 +191,7 @@
                 at = (part * 4 + slot) * 128
                 left_ref[at:at + 128, :] = jnp.concatenate([high, low, high, low], axis=1)
 
-    high, low = split(ritz_ref[...])
+    high, low = split(jnp.concatenate([ritz_ref[k] for k in range(ritz_ref.shape[0])], axis=0))
     right = jnp.concatenate([high, high, low, low], axis=0)
     for part in range(2):
         out_ref[part] = (base_ref[part].astype(F32)
@@ -206,21 +206,19 @@
         grid=(base.shape[2] // COLUMNS,),
         out_shape=[jax.ShapeDtypeStruct(base.shape, BF16), jax.ShapeDtypeStruct(applied.shape, F32)],
         in_specs=[once(coef), once(image), once(applied),
-                  pl.BlockSpec((ritz.shape[0], COLUMNS), lambda j: (0, j)), slab],
+                  pl.BlockSpec(ritz.shape[:2] + (COLUMNS,), lambda j: (0, 0, j)), slab],
         out_specs=[slab, once(applied)],
         scratch_shapes=[pltpu.VMEM((1024, 512), BF16)],
-        compiler_params=pltpu.CompilerParams(vmem_limit_bytes=56 * 2**20),
+        compiler_params=pltpu.CompilerParams(vmem_limit_bytes=LIMIT),
         name="rotate",
     )(coef, image, applied, ritz, base)
 
 
-def greet(n_tg, n_pool, tg, pool):
+def greet(axis, size, me):
     barrier = pltpu.get_barrier_semaphore()
-    for step in range(1, n_tg):
-        pl.semaphore_signal(barrier, inc=1, device_id={"tg": lax.rem(tg + step, n_tg)}, device_id_type=MESH)
-    for step in range(1, n_pool):
-        pl.semaphore_signal(barrier, inc=1, device_id={"pool": lax.rem(pool + step, n_pool)}, device_id_type=MESH)
-    pl.semaphore_wait(barrier, n_tg + n_pool - 2)
+    for step in range(1, size):
+        pl.semaphore_signal(barrier, inc=1, device_id={axis: lax.rem(me + step, size)}, device_id_type=MESH)
+    return barrier
 
 
 class Exchange:
@@ -264,16 +262,18 @@
             pack_ref[k, j] = flat_ref[pl.ds(k * 4 + j, 8, 64), :]
 
 
-def spread_kernel(n_tg, n_pool, wave_hbm, count_hbm, table_hbm, ritz_hbm,
-                  planes_ref, coef_ref, usable_ref, ritz_ref,
-                  wave_ref, count_ref, table_ref, rows_ref, flat_ref, sticks_ref, pack_ref,
-                  send_t, recv_t, send_p, recv_p, own_sem, load_sem):
-    tg, pool = lax.axis_index("tg"), lax.axis_index("pool")
-    pairs = [(count_hbm, count_ref), (wave_hbm, wave_ref), (table_hbm, table_ref), (ritz_hbm, rows_ref)]
+def spread_kernel(n_tg, n_pool, wave_hbm, count_hbm, planes_ref, pack_ref, usable_ref, cs_ref,
+                  wave_ref, count_ref, table_ref, flat_ref, sticks_ref, send_t, recv_t, own_sem, load_sem):
+    tg = lax.axis_index("tg")
+    pairs = [(count_hbm, count_ref), (wave_hbm, wave_ref)]
     loads = [pltpu.make_async_copy(src, dst, load_sem.at[k]) for k, (src, dst) in enumerate(pairs)]
     for load in loads:
         load.start()
-    greet(n_tg, n_pool, tg, pool)
+    barrier = greet("tg", n_tg, tg)
+    cs = cos_sin()
+    for k in range(4):
+        cs_ref[k] = cs[k]
+    table_ref[...] = as_rhs_rows(cs, 1)
     for load in loads:
         load.wait()
     slot = lax.broadcasted_iota(jnp.int32, (64, 128), 0)
@@ -290,29 +290,33 @@
         sticks_ref[t] = jnp.concatenate(
             [res[band * 64:(band + 1) * 64, part * 128 + t * 16:part * 128 + t * 16 + 16]
              for part in range(2) for band in range(4)], axis=1)
+    pl.semaphore_wait(barrier, n_tg - 1)
     planes = Exchange("tg", n_tg, tg, sticks_ref, planes_ref, send_t, recv_t, own_sem.at[0])
     planes.start()
     pack_rows(flat_ref, pack_ref, n_pool)
-    coef = Exchange("pool", n_pool, pool, pack_ref, coef_ref, send_p, recv_p, own_sem.at[1])
+    planes.wait_recv()
+    planes.wait_send()
+
+
+def collect_kernel(n_tg, n_pool, cols_hbm, usable_hbm, cs_hbm, pack_hbm, applied_ref, image_ref, coef_ref,
+                   usable_ref, cs_ref, table_ref, returned_ref, pack_ref,
+                   send_t, recv_t, send_p, recv_p, send_c, recv_c, own_sem, load_sem):
+    tg, pool = lax.axis_index("tg"), lax.axis_index("pool")
+    pairs = [(usable_hbm, usable_ref), (cs_hbm, cs_ref)]
+    loads = [pltpu.make_async_copy(src, dst, load_sem.at[k]) for k, (src, dst) in enumerate(pairs)]
+    for load in loads:
+        load.start()
+    barrier = greet("tg", n_tg, tg)
+    greet("pool", n_pool, pool)
+    pl.semaphore_wait(barrier, n_tg + n_pool - 2)
+    back = Exchange("tg", n_tg, tg, cols_hbm, returned_ref, send_t, recv_t, own_sem.at[0])
+    back.start()
+    coef = Exchange("pool", n_pool, pool, pack_hbm, coef_ref, send_c, recv_c, own_sem.at[2])
     coef.start()
-    for term in range(2):
-        ritz_ref[term * 4:term * 4 + 4, :] = rows_ref[term]
-    planes.wait_recv()
-    coef.wait_recv()
-    planes.wait_send()
-    coef.wait_send()
-
-
-def collect_kernel(n_tg, n_pool, cols_ref, usable_ref, table_hbm, applied_ref, image_ref,
-                   table_ref, returned_ref, pack_ref, send_t, recv_t, send_p, recv_p, own_sem, load_sem):
-    tg, pool = lax.axis_index("tg"), lax.axis_index("pool")
-    load = pltpu.make_async_copy(table_hbm, table_ref, load_sem.at[0])
-    load.start()
-    greet(n_tg, n_pool, tg, pool)
-    back = Exchange("tg", n_tg, tg, cols_ref, returned_ref, send_t, recv_t, own_sem.at[0])
-    back.start()
+    for load in loads:
+        load.wait()
     usable = usable_ref[...]
-    load.wait()
+    table_ref[...] = as_rhs_rows([cs_ref[k] for k in range(4)], -1)
     back.wait_recv()
     rows = []
     for band in range(4):
@@ -327,60 +331,57 @@
     pack_rows(applied_ref, pack_ref, n_pool)
     image = Exchange("pool", n_pool, pool, pack_ref, image_ref, send_p, recv_p, own_sem.at[1])
     image.start()
+    coef.wait_recv()
     image.wait_recv()
     back.wait_send()
+    coef.wait_send()
     image.wait_send()
 
 
-def exchange_scratch(n_tg, n_pool):
-    dma = pltpu.SemaphoreType.DMA
-    return [dma((n_tg,)), dma((n_tg,)), dma((n_pool,)), dma((n_pool,)), dma((2,))]
-
-
-def spread(wave, count, ritz, n_tg, n_pool):
+def spread(wave, count, n_tg, n_pool):
     vmem = pl.BlockSpec(memory_space=pltpu.VMEM)
     hbm = pl.BlockSpec(memory_space=pltpu.HBM)
+    dma = pltpu.SemaphoreType.DMA
     return pl.pallas_call(
         functools.partial(spread_kernel, n_tg, n_pool),
         out_shape=[jax.ShapeDtypeStruct((n_tg, 64, 128), F32), jax.ShapeDtypeStruct((n_pool, 4, 8, 128), F32),
-                   jax.ShapeDtypeStruct((64, 128), F32), jax.ShapeDtypeStruct((8, ritz.shape[2]), F32)],
-        in_specs=[hbm] * 4,
+                   jax.ShapeDtypeStruct((64, 128), F32), jax.ShapeDtypeStruct((4, 128, 128), BF16)],
+        in_specs=[hbm] * 2,
         out_specs=[vmem] * 4,
         scratch_shapes=[pltpu.VMEM(wave.shape, F32), pltpu.SMEM(count.shape, jnp.int32),
-                        pltpu.VMEM((768, 256), BF16), pltpu.VMEM(ritz.shape, F32),
-                        pltpu.VMEM((512, 128), F32), pltpu.VMEM((n_tg, 64, 128), F32),
-                        pltpu.VMEM((n_pool, 4, 8, 128), F32)] + exchange_scratch(n_tg, n_pool)
-        + [pltpu.SemaphoreType.DMA((4,))],
-        compiler_params=pltpu.CompilerParams(collective_id=0, has_side_effects=True,
-                                             vmem_limit_bytes=48 * 2**20),
+                        pltpu.VMEM((768, 256), BF16), pltpu.VMEM((512, 128), F32),
+                        pltpu.VMEM((n_tg, 64, 128), F32), dma((n_tg,)), dma((n_tg,)), dma((1,)), dma((2,))],
+        compiler_params=pltpu.CompilerParams(collective_id=0, has_side_effects=True, vmem_limit_bytes=LIMIT),
         name="spread",
-    )(wave, count, as_rhs_rows(row_table(128, 1.0)), ritz)
-
-
-def collect(columns, usable, n_tg, n_pool):
+    )(wave, count)
+
+
+def collect(columns, usable, cs, pack, n_tg, n_pool):
     vmem = pl.BlockSpec(memory_space=pltpu.VMEM)
     hbm = pl.BlockSpec(memory_space=pltpu.HBM)
+    dma = pltpu.SemaphoreType.DMA
     return pl.pallas_call(
         functools.partial(collect_kernel, n_tg, n_pool),
-        out_shape=[jax.ShapeDtypeStruct((512, 128), F32), jax.ShapeDtypeStruct((n_pool, 4, 8, 128), F32)],
-        in_specs=[vmem, vmem, hbm],
-        out_specs=[vmem] * 2,
-        scratch_shapes=[pltpu.VMEM((768, 256), BF16), pltpu.VMEM((n_tg, 64, 128), F32),
-                        pltpu.VMEM((n_pool, 4, 8, 128), F32)] + exchange_scratch(n_tg, n_pool)
-        + [pltpu.SemaphoreType.DMA((1,))],
-        compiler_params=pltpu.CompilerParams(collective_id=1, has_side_effects=True,
-                                             vmem_limit_bytes=48 * 2**20),
+        out_shape=[jax.ShapeDtypeStruct((512, 128), F32), jax.ShapeDtypeStruct(pack.shape, F32),
+                   jax.ShapeDtypeStruct(pack.shape, F32)],
+        in_specs=[hbm] * 4,
+        out_specs=[vmem, hbm, hbm],
+        scratch_shapes=[pltpu.VMEM(usable.shape, F32), pltpu.VMEM(cs.shape, BF16), pltpu.VMEM((768, 256), BF16),
+                        pltpu.VMEM((n_tg, 64, 128), F32), pltpu.VMEM(pack.shape, F32),
+                        dma((n_tg,)), dma((n_tg,)), dma((n_pool,)), dma((n_pool,)), dma((n_pool,)), dma((n_pool,)),
+                        dma((3,)), dma((2,))],
+        compiler_params=pltpu.CompilerParams(collective_id=1, has_side_effects=True, vmem_limit_bytes=LIMIT),
         name="collect",
-    )(columns, usable, as_rhs_rows(row_table(128, -1.0)))
+    )(columns, usable, cs, pack)
 
 
 def local(wave_coef, potential, stick_pos, stick_count, ritz_block, slab_base):
     n_tg, n_pool = lax.axis_size("tg"), lax.axis_size("pool")
     slots = wave_coef.shape[2]
-    planes, coef, usable, ritz_rows = spread(wave_coef, stick_count, ritz_block, n_tg, n_pool)
-    ritz_full = lax.all_gather(ritz_rows, "pool", axis=0, tiled=True)
-    columns = plane_step(planes.reshape(n_tg * slots, 128), stick_pos, potential)
-    applied, image = collect(columns.reshape(n_tg, slots, 128), usable, n_tg, n_pool)
+    ritz_full = lax.all_gather(ritz_block, "pool", axis=0, tiled=True)
+    planes, pack, usable, cs = spread(wave_coef, stick_count, n_tg, n_pool)
+    columns = plane_step(planes.reshape(n_tg * slots, 128), stick_pos, cs, potential)
+    applied, image, coef = collect(columns.reshape(n_tg, slots, 128), usable, cs, pack, n_tg, n_pool)
     rotated, applied = rotate(coef, image, ritz_full, slab_base, applied)
     return applied.reshape(wave_coef.shape), rotated
 

time: 94.9 us -> 83.5 us (0.88)
  local copies, waits for them, and re-layouts: 10.3 us -> 0 us
  Pallas kernels: 69.9 us -> 68.3 us
    unnamed x24 -> x0, local copies, waits for them, and re-layouts: 10.3 us -> none
    pallas_call x1, Pallas kernels: 17.9 us -> 11.6 us  [spread(): pl.pallas_call(functools.partial(spread_kernel, n_tg, n_pool), out_shape=...]
    pallas_call x1, Pallas kernels: 16.2 us -> 20.2 us  [collect(): pl.pallas_call(functools.partial(collect_kernel, n_tg, n_pool), out_shape...]
  transfers between devices with their start and end apart: 1 -> 1, of which waited for: 0 -> 0; matrix products, arithmetic and copies ran while one was open for 0% -> 0% of each run, Pallas kernels for 43% -> 68%
where the time goes in v3:
time: 83.5 us; the launch traced here: 83.1 us
  Pallas kernels  68.3 us (82%)
  between operations  14.1 us (17%)
    pallas_call x1, Pallas kernels, plane_step(): pl.pallas_call(plane_kernel, out_shape=jax.ShapeDtypeStruct((slots, 128),...  24.8 us
    pallas_call x1, Pallas kernels, collect(): pl.pallas_call(functools.partial(collect_kernel, n_tg, n_pool), out_shape...  20.2 us
    pallas_call x1, Pallas kernels, rotate(): pl.pallas_call(rotate_kernel, grid=(base.shape[2] // COLUMNS,), out_shape...  11.8 us
    pallas_call x1, Pallas kernels, spread(): pl.pallas_call(functools.partial(spread_kernel, n_tg, n_pool), out_shape=...  11.6 us
  transfers between devices with their start and end apart: 1, of which 0 were waited for; matrix products, arithmetic and copies ran while one was open for 0% of the time, Pallas kernels for 68%

profile of v3, /device:TPU:1, one launch (start us, length us, event | category | flops | bytes accessed | tf_op | source)
XLA Modules:
  0.0 83.1 jit_solution(14143050924189065765)
XLA Ops:
  7.2 0.0 all-gather.2.cloned.1.call-start
  7.2 0.7 all-gather.2.cloned.1.call-update
  7.9 11.6 %spread.1 = (f32[8,64,128]{2,1,0:T(8,128)}, f32[16,4,8,128]{3,2,1,0:T(8,128)}, f32[64,128]{1,0:T(8,128)}, bf16[4,128,128]{2,1,0:T(8,128)(2,1)}) custom-call(f32[2,4,64,128]{3,2,1,0:T(8,128)} %wave_hbm.1, s32[8]{0:T(128)} %count_hbm.1), custom_call_target="tpu_custom_call" | custom-call | tf_op jit(solution)/shard_map/spread/pallas_call | solution.py:345
  19.5 24.8 %planes.1 = f32[512,128]{1,0:T(8,128)} custom-call(s32[512]{0:T(512)} %pos_hbm.1, f32[512,128]{1,0:T(8,128)} %bitcast.4, bf16[4,128,128]{2,1,0:T(8,128)(2,1)} %get-tuple-element.12.cs_hbm, f32[16,128,128]{2,1,0:T(8,128)} %pot_hbm.1), custom_call_target="tpu_custom_call" | custom-call | tf_op jit(solution)/shard_map/planes/pallas_call | solution.py:155
  44.3 20.2 %collect.1 = (f32[512,128]{1,0:T(8,128)}, f32[16,4,8,128]{3,2,1,0:T(8,128)}, f32[16,4,8,128]{3,2,1,0:T(8,128)}) custom-call(f32[8,64,128]{2,1,0:T(8,128)} %bitcast.3, f32[64,128]{1,0:T(8,128)} %get-tuple-element.13.usable_hbm, bf16[4,128,128]{2,1,0:T(8,128)(2,1)} %get-tuple-element.12.cs_hbm, f32[16,4,8,128]{3,2,1,0:T(8,128)} %get-tuple-element.14.pack_hbm), custom_call_target="tpu_custom_call" | custom-call | tf_op jit(solution)/shard_map/collect/pallas_call | solution.py:363
  64.4 0.0 all-gather.2.cloned.1.call-done.ritz_ref
  64.5 11.8 %rotate.1 = (bf16[2,512,4096]{2,1,0:T(8,128)(2,1)}, f32[512,128]{1,0:T(8,128)}) custom-call(f32[16,4,8,128]{3,2,1,0:T(8,128)} %get-tuple-element.15.coef_ref, f32[16,4,8,128]{3,2,1,0:T(8,128)} %get-tuple-element.16.image_ref, f32[512,128]{1,0:T(8,128)} %get-tuple-element.17.applied_ref, f32[32,4,4096]{2,1,0:T(4,128)} %all-gather.2.cloned.1.call-done.ritz_ref, ...), custom_call_target="tpu_custom_call" | custom-call | tf_op jit(solution)/shard_map/rotate/pallas_call | solution.py:204
Async XLA Ops:
  7.2 57.3 %all-gather.2.cloned.1.call-start = ((), (), s32[]{:S(2)}) async-start(), calls=%async_computation | async-start | bytes 2228224 | tf_op jit(solution)/shard_map/all_gather | solution.py:381
Sparse Core Ops, SparseCore 0:
  9.7 37.9 all-gather.1

commit v4 on v3

--- a/solution.py
+++ b/solution.py
@@ -72,12 +72,16 @@
 X_STEP = 2
 
 
-def plane_kernel(pos_hbm, sticks_hbm, cs_hbm, pot_hbm,
-                 out_ref, pos_ref, sticks_ref, cs_ref, pot_ref, ty_ref, ax_ref, bx_ref,
-                 grid_ref, re_ref, im_ref, sems):
+def chunk(ref, step):
+    rows = Y_STEP * PITCH
+    return ref.at[pl.ds(pl.multiple_of(step * rows, 8), rows), :]
+
+
+def lattice_kernel(pos_hbm, sticks_hbm, cs_hbm, re_hbm, im_hbm,
+                   pos_ref, sticks_ref, cs_ref, ty_ref, grid_ref, re_ref, im_ref, sems, out_sems):
     slots = sticks_ref.shape[0]
     half = 64
-    pairs = [(pos_hbm, pos_ref), (sticks_hbm, sticks_ref), (cs_hbm, cs_ref), (pot_hbm, pot_ref)]
+    pairs = [(pos_hbm, pos_ref), (sticks_hbm, sticks_ref), (cs_hbm, cs_ref)]
     copies = [pltpu.make_async_copy(src, dst, sems.at[k]) for k, (src, dst) in enumerate(pairs)]
     for copy in copies:
         copy.start()
@@ -87,10 +91,7 @@
         grid_ref[pl.ds(pl.multiple_of(x * 512, 512), 512), :] = jnp.zeros((512, 128), F32)
 
     copies[2].wait()
-    cs = [cs_ref[k] for k in range(4)]
-    ty_ref[...] = as_rhs_rows(cs, 1)
-    ax_ref[...] = as_lhs(cs, 1) * (1.0 / 128.0 ** 3)
-    bx_ref[...] = as_lhs(cs, -1)
+    ty_ref[...] = as_rhs_rows([cs_ref[k] for k in range(4)], 1)
     copies[0].wait()
     copies[1].wait()
 
@@ -100,6 +101,10 @@
         rows = sticks_ref[pl.ds(base, 8), :]
         for k in range(8):
             grid_ref[pl.ds(pos_ref[base + k], 1), :] = rows[k:k + 1, :]
+
+    def stores(step):
+        return [pltpu.make_async_copy(chunk(src, step), chunk(dst, step), out_sems.at[k, step])
+                for k, (src, dst) in enumerate([(re_ref, re_hbm), (im_ref, im_hbm)])]
 
     @pl.loop(0, 128 // Y_STEP)
     def _(step):
@@ -113,9 +118,40 @@
             to = pl.ds((step * Y_STEP + k) * PITCH, half)
             re_ref[to, :] = res[k * half:(k + 1) * half, :128]
             im_ref[to, :] = res[k * half:(k + 1) * half, 128:]
-
-    copies[3].wait()
-
+        for store in stores(step):
+            store.start()
+
+    @pl.loop(0, 128 // Y_STEP)
+    def _(step):
+        for store in stores(step):
+            store.wait()
+
+
+def lattice(sticks, stick_pos, cs):
+    hbm = pl.BlockSpec(memory_space=pltpu.HBM)
+    size = (128 * PITCH, 128)
+    return pl.pallas_call(
+        lattice_kernel,
+        out_shape=[jax.ShapeDtypeStruct(size, F32)] * 2,
+        in_specs=[hbm] * 3,
+        out_specs=[hbm] * 2,
+        scratch_shapes=[
+            pltpu.SMEM(stick_pos.shape, jnp.int32),
+            pltpu.VMEM(sticks.shape, F32),
+            pltpu.VMEM(cs.shape, BF16),
+            pltpu.VMEM((768, 256), BF16),
+            pltpu.VMEM((16384, 128), F32),
+            pltpu.VMEM(size, F32),
+            pltpu.VMEM(size, F32),
+            pltpu.SemaphoreType.DMA((3,)),
+            pltpu.SemaphoreType.DMA((2, 128 // Y_STEP)),
+        ],
+        compiler_params=pltpu.CompilerParams(vmem_limit_bytes=LIMIT),
+        name="lattice",
+    )(stick_pos, sticks, cs)
+
+
+def x_transforms(pot_ref, ax_ref, bx_ref, re_ref, im_ref):
     @pl.loop(0, 16, unroll=2)
     def _(z):
         pot = pot_ref[z]
@@ -131,6 +167,10 @@
                 re_ref[at[k], :] = back[:128, k * 128:(k + 1) * 128]
                 im_ref[at[k], :] = back[128:, k * 128:(k + 1) * 128]
 
+
+def y_transform_back(bx_ref, re_ref, im_ref, grid_ref):
+    half = 64
+
     @pl.loop(0, 128 // Y_STEP)
     def _(step):
         data = jnp.concatenate(
@@ -142,38 +182,6 @@
             grid_ref[to, :] = jnp.concatenate(
                 [res[:128, k * half:(k + 1) * half], res[128:, k * half:(k + 1) * half]], axis=1)
 
-    @pl.loop(0, slots // 8)
-    def _(block):
-        base = pl.multiple_of(block * 8, 8)
-        out_ref[pl.ds(base, 8), :] = jnp.concatenate(
-            [grid_ref[pl.ds(pos_ref[base + k], 1), :] for k in range(8)], axis=0)
-
-
-def plane_step(sticks, stick_pos, cs, pot):
-    slots = sticks.shape[0]
-    hbm = pl.BlockSpec(memory_space=pltpu.HBM)
-    return pl.pallas_call(
-        plane_kernel,
-        out_shape=jax.ShapeDtypeStruct((slots, 128), F32),
-        in_specs=[hbm] * 4,
-        out_specs=pl.BlockSpec(memory_space=pltpu.VMEM),
-        scratch_shapes=[
-            pltpu.SMEM((slots,), jnp.int32),
-            pltpu.VMEM(sticks.shape, F32),
-            pltpu.VMEM(cs.shape, BF16),
-            pltpu.VMEM((16, 128, 128), F32),
-            pltpu.VMEM((768, 256), BF16),
-            pltpu.VMEM((256, 768), BF16),
-            pltpu.VMEM((256, 768), BF16),
-            pltpu.VMEM((16384, 128), F32),
-            pltpu.VMEM((128 * PITCH, 128), F32),
-            pltpu.VMEM((128 * PITCH, 128), F32),
-            pltpu.SemaphoreType.DMA((4,)),
-        ],
-        compiler_params=pltpu.CompilerParams(vmem_limit_bytes=LIMIT),
-        name="planes",
-    )(stick_pos, sticks, cs, pot)
-
 
 COLUMNS = 512
 
@@ -185,7 +193,8 @@
         for part in range(2):
             for slot in range(4):
                 rows = jnp.concatenate(
-                    [ref[k, slot, part * 4:part * 4 + 4, :] for k in range(16) for ref in (coef_ref, image_ref)],
+                    [ref[(y * 4 + z) * 2 + core, slot, part * 4:part * 4 + 4, :]
+                     for y in range(2) for core in range(2) for z in range(4) for ref in (coef_ref, image_ref)],
                     axis=0).T
                 high, low = split(rows)
                 at = (part * 4 + slot) * 128
@@ -237,10 +246,14 @@
     def own(self):
         return pltpu.make_async_copy(self.source.at[self.me], self.target.at[self.me], self.own_sem)
 
-    def start(self):
-        for step in range(1, self.size):
-            self.remote(step).start()
-        self.own().start()
+    def start(self, prepare=None):
+        for step in range(1, self.size + 1):
+            if prepare is not None:
+                prepare(lax.rem(self.me + step, self.size))
+            if step < self.size:
+                self.remote(step).start()
+            else:
+                self.own().start()
 
     def wait_recv(self):
         self.own().wait()
@@ -262,20 +275,39 @@
             pack_ref[k, j] = flat_ref[pl.ds(k * 4 + j, 8, 64), :]
 
 
-def spread_kernel(n_tg, n_pool, wave_hbm, count_hbm, planes_ref, pack_ref, usable_ref, cs_ref,
-                  wave_ref, count_ref, table_ref, flat_ref, sticks_ref, send_t, recv_t, own_sem, load_sem):
-    tg = lax.axis_index("tg")
-    pairs = [(count_hbm, count_ref), (wave_hbm, wave_ref)]
+def pool_parts(pool):
+    return pool // 8, lax.rem(pool // 2, 4), lax.rem(pool, 2)
+
+
+def pool_index(y, z, core):
+    return (y * 4 + z) * 2 + core
+
+
+def remote(src, dst, send, recv, **peer):
+    return pltpu.make_async_remote_copy(src_ref=src, dst_ref=dst, send_sem=send, recv_sem=recv,
+                                        device_id=peer, device_id_type=MESH)
+
+
+def spread_kernel(n_tg, n_pool, wave_hbm, count_hbm, ritz_hbm, planes_ref, pack_ref, usable_ref, cs_ref, col_hbm,
+                  wave_ref, count_ref, table_ref, flat_ref, sticks_ref, send_t, recv_t, own_sem, load_sem,
+                  send_r, recv_r):
+    tg, pool = lax.axis_index("tg"), lax.axis_index("pool")
+    y, z, core = pool_parts(pool)
+    after, before, across = lax.rem(z + 1, 4), lax.rem(z + 3, 4), lax.rem(z + 2, 4)
+    up, down = pool_index(y, after, core), pool_index(y, before, core)
+    pairs = [(count_hbm, count_ref), (wave_hbm, wave_ref), (ritz_hbm, col_hbm.at[z])]
     loads = [pltpu.make_async_copy(src, dst, load_sem.at[k]) for k, (src, dst) in enumerate(pairs)]
     for load in loads:
         load.start()
     barrier = greet("tg", n_tg, tg)
+    for peer in (up, down):
+        pl.semaphore_signal(barrier, inc=1, device_id={"pool": peer}, device_id_type=MESH)
     cs = cos_sin()
     for k in range(4):
         cs_ref[k] = cs[k]
     table_ref[...] = as_rhs_rows(cs, 1)
-    for load in loads:
-        load.wait()
+    loads[0].wait()
+    loads[1].wait()
     slot = lax.broadcasted_iota(jnp.int32, (64, 128), 0)
     usable = jnp.where(slot < count_ref[tg], 1.0, 0.0).astype(F32)
     usable_ref[...] = usable
@@ -290,33 +322,77 @@
         sticks_ref[t] = jnp.concatenate(
             [res[band * 64:(band + 1) * 64, part * 128 + t * 16:part * 128 + t * 16 + 16]
              for part in range(2) for band in range(4)], axis=1)
-    pl.semaphore_wait(barrier, n_tg - 1)
+    pl.semaphore_wait(barrier, n_tg + 1)
     planes = Exchange("tg", n_tg, tg, sticks_ref, planes_ref, send_t, recv_t, own_sem.at[0])
     planes.start()
+    rise = remote(ritz_hbm, col_hbm.at[z], send_r.at[0], recv_r.at[0], pool=up)
+    fall = remote(ritz_hbm, col_hbm.at[z], send_r.at[1], recv_r.at[1], pool=down)
+    rise.start()
+    fall.start()
     pack_rows(flat_ref, pack_ref, n_pool)
+    remote(ritz_hbm, col_hbm.at[before], send_r.at[0], recv_r.at[0], pool=up).wait_recv()
+    rise_on = remote(col_hbm.at[before, 0], col_hbm.at[before, 0], send_r.at[2], recv_r.at[2], pool=up)
+    rise_on.start()
+    remote(ritz_hbm, col_hbm.at[after], send_r.at[1], recv_r.at[1], pool=down).wait_recv()
+    fall_on = remote(col_hbm.at[after, 1], col_hbm.at[after, 1], send_r.at[3], recv_r.at[3], pool=down)
+    fall_on.start()
     planes.wait_recv()
+    remote(col_hbm.at[before, 0], col_hbm.at[across, 0], send_r.at[2], recv_r.at[2], pool=up).wait_recv()
+    remote(col_hbm.at[after, 1], col_hbm.at[across, 1], send_r.at[3], recv_r.at[3], pool=down).wait_recv()
+    loads[2].wait()
     planes.wait_send()
-
-
-def collect_kernel(n_tg, n_pool, cols_hbm, usable_hbm, cs_hbm, pack_hbm, applied_ref, image_ref, coef_ref,
-                   usable_ref, cs_ref, table_ref, returned_ref, pack_ref,
-                   send_t, recv_t, send_p, recv_p, send_c, recv_c, own_sem, load_sem):
+    for copy in (rise, fall, rise_on, fall_on):
+        copy.wait_send()
+
+
+def collect_kernel(n_tg, n_pool, pos_hbm, re_hbm, im_hbm, pot_hbm, usable_hbm, cs_hbm, pack_hbm, col_hbm,
+                   applied_ref, image_ref, coef_ref, ritz_ref,
+                   pos_ref, re_ref, im_ref, pot_ref, usable_ref, cs_ref,
+                   ax_ref, bx_ref, table_ref, grid_ref, cols_ref, returned_ref, pack_ref,
+                   send_t, recv_t, send_p, recv_p, send_c, recv_c, own_sem, load_sem, send_r, recv_r):
     tg, pool = lax.axis_index("tg"), lax.axis_index("pool")
-    pairs = [(usable_hbm, usable_ref), (cs_hbm, cs_ref)]
+    y, z, core = pool_parts(pool)
+    pairs = [(cs_hbm, cs_ref), (re_hbm, re_ref), (im_hbm, im_ref), (pot_hbm, pot_ref),
+             (usable_hbm, usable_ref), (pos_hbm, pos_ref), (col_hbm, ritz_ref.at[y, core])]
     loads = [pltpu.make_async_copy(src, dst, load_sem.at[k]) for k, (src, dst) in enumerate(pairs)]
     for load in loads:
         load.start()
     barrier = greet("tg", n_tg, tg)
     greet("pool", n_pool, pool)
+    loads[0].wait()
+    cs = [cs_ref[k] for k in range(4)]
+    ax_ref[...] = as_lhs(cs, 1) * (1.0 / 128.0 ** 3)
+    bx_ref[...] = as_lhs(cs, -1)
+    table_ref[...] = as_rhs_rows(cs, -1)
     pl.semaphore_wait(barrier, n_tg + n_pool - 2)
-    back = Exchange("tg", n_tg, tg, cols_hbm, returned_ref, send_t, recv_t, own_sem.at[0])
-    back.start()
+    next_core = pool_index(y, z, 1 - core)
+    next_y = pool_index(1 - y, z, core)
+    to_y = remote(col_hbm, ritz_ref.at[y, core], send_r.at[0], recv_r.at[0], pool=next_y)
+    to_core = remote(col_hbm, ritz_ref.at[y, core], send_r.at[1], recv_r.at[1], pool=next_core)
+    to_y.start()
+    to_core.start()
     coef = Exchange("pool", n_pool, pool, pack_hbm, coef_ref, send_c, recv_c, own_sem.at[2])
     coef.start()
-    for load in loads:
+    for load in loads[1:4]:
         load.wait()
+    x_transforms(pot_ref, ax_ref, bx_ref, re_ref, im_ref)
+    remote(col_hbm, ritz_ref.at[1 - y, core], send_r.at[0], recv_r.at[0], pool=next_y).wait_recv()
+    on_core = remote(ritz_ref.at[1 - y, core], ritz_ref.at[1 - y, core], send_r.at[2], recv_r.at[2], pool=next_core)
+    on_core.start()
+    y_transform_back(bx_ref, re_ref, im_ref, grid_ref)
+    loads[4].wait()
+    loads[5].wait()
+
+    def gather(peer):
+        @pl.loop(0, 8)
+        def _(block):
+            base = pl.multiple_of(block * 8, 8)
+            cols_ref[peer, pl.ds(base, 8), :] = jnp.concatenate(
+                [grid_ref[pl.ds(pos_ref[peer * 64 + base + k], 1), :] for k in range(8)], axis=0)
+
+    back = Exchange("tg", n_tg, tg, cols_ref, returned_ref, send_t, recv_t, own_sem.at[0])
+    back.start(gather)
     usable = usable_ref[...]
-    table_ref[...] = as_rhs_rows([cs_ref[k] for k in range(4)], -1)
     back.wait_recv()
     rows = []
     for band in range(4):
@@ -332,57 +408,67 @@
     image = Exchange("pool", n_pool, pool, pack_ref, image_ref, send_p, recv_p, own_sem.at[1])
     image.start()
     coef.wait_recv()
+    loads[6].wait()
+    remote(col_hbm, ritz_ref.at[y, 1 - core], send_r.at[1], recv_r.at[1], pool=next_core).wait_recv()
+    remote(ritz_ref.at[1 - y, core], ritz_ref.at[1 - y, 1 - core], send_r.at[2], recv_r.at[2],
+           pool=next_core).wait_recv()
     image.wait_recv()
-    back.wait_send()
-    coef.wait_send()
-    image.wait_send()
-
-
-def spread(wave, count, n_tg, n_pool):
+    for exchange in (back, coef, image):
+        exchange.wait_send()
+    for copy in (to_y, to_core, on_core):
+        copy.wait_send()
+
+
+def spread(wave, count, ritz, n_tg, n_pool):
     vmem = pl.BlockSpec(memory_space=pltpu.VMEM)
     hbm = pl.BlockSpec(memory_space=pltpu.HBM)
     dma = pltpu.SemaphoreType.DMA
     return pl.pallas_call(
         functools.partial(spread_kernel, n_tg, n_pool),
         out_shape=[jax.ShapeDtypeStruct((n_tg, 64, 128), F32), jax.ShapeDtypeStruct((n_pool, 4, 8, 128), F32),
-                   jax.ShapeDtypeStruct((64, 128), F32), jax.ShapeDtypeStruct((4, 128, 128), BF16)],
-        in_specs=[hbm] * 2,
-        out_specs=[vmem] * 4,
+                   jax.ShapeDtypeStruct((64, 128), F32), jax.ShapeDtypeStruct((4, 128, 128), BF16),
+                   jax.ShapeDtypeStruct((4,) + ritz.shape, F32)],
+        in_specs=[hbm] * 3,
+        out_specs=[vmem] * 4 + [hbm],
         scratch_shapes=[pltpu.VMEM(wave.shape, F32), pltpu.SMEM(count.shape, jnp.int32),
                         pltpu.VMEM((768, 256), BF16), pltpu.VMEM((512, 128), F32),
-                        pltpu.VMEM((n_tg, 64, 128), F32), dma((n_tg,)), dma((n_tg,)), dma((1,)), dma((2,))],
+                        pltpu.VMEM((n_tg, 64, 128), F32), dma((n_tg,)), dma((n_tg,)), dma((1,)), dma((3,)),
+                        dma((4,)), dma((4,))],
         compiler_params=pltpu.CompilerParams(collective_id=0, has_side_effects=True, vmem_limit_bytes=LIMIT),
         name="spread",
-    )(wave, count)
-
-
-def collect(columns, usable, cs, pack, n_tg, n_pool):
+    )(wave, count, ritz)
+
+
+def collect(stick_pos, re, im, pot, usable, cs, pack, col, n_tg, n_pool):
     vmem = pl.BlockSpec(memory_space=pltpu.VMEM)
     hbm = pl.BlockSpec(memory_space=pltpu.HBM)
     dma = pltpu.SemaphoreType.DMA
     return pl.pallas_call(
         functools.partial(collect_kernel, n_tg, n_pool),
         out_shape=[jax.ShapeDtypeStruct((512, 128), F32), jax.ShapeDtypeStruct(pack.shape, F32),
-                   jax.ShapeDtypeStruct(pack.shape, F32)],
-        in_specs=[hbm] * 4,
-        out_specs=[vmem, hbm, hbm],
-        scratch_shapes=[pltpu.VMEM(usable.shape, F32), pltpu.VMEM(cs.shape, BF16), pltpu.VMEM((768, 256), BF16),
+                   jax.ShapeDtypeStruct(pack.shape, F32), jax.ShapeDtypeStruct((2, 2) + col.shape, F32)],
+        in_specs=[hbm] * 8,
+        out_specs=[vmem, hbm, hbm, hbm],
+        scratch_shapes=[pltpu.SMEM(stick_pos.shape, jnp.int32), pltpu.VMEM(re.shape, F32), pltpu.VMEM(im.shape, F32),
+                        pltpu.VMEM(pot.shape, F32), pltpu.VMEM(usable.shape, F32), pltpu.VMEM(cs.shape, BF16),
+                        pltpu.VMEM((256, 768), BF16), pltpu.VMEM((256, 768), BF16), pltpu.VMEM((768, 256), BF16),
+                        pltpu.VMEM((16384, 128), F32), pltpu.VMEM((n_tg, 64, 128), F32),
                         pltpu.VMEM((n_tg, 64, 128), F32), pltpu.VMEM(pack.shape, F32),
                         dma((n_tg,)), dma((n_tg,)), dma((n_pool,)), dma((n_pool,)), dma((n_pool,)), dma((n_pool,)),
-                        dma((3,)), dma((2,))],
+                        dma((3,)), dma((7,)), dma((3,)), dma((3,))],
         compiler_params=pltpu.CompilerParams(collective_id=1, has_side_effects=True, vmem_limit_bytes=LIMIT),
         name="collect",
-    )(columns, usable, cs, pack)
+    )(stick_pos, re, im, pot, usable, cs, pack, col)
 
 
 def local(wave_coef, potential, stick_pos, stick_count, ritz_block, slab_base):
     n_tg, n_pool = lax.axis_size("tg"), lax.axis_size("pool")
     slots = wave_coef.shape[2]
-    ritz_full = lax.all_gather(ritz_block, "pool", axis=0, tiled=True)
-    planes, pack, usable, cs = spread(wave_coef, stick_count, n_tg, n_pool)
-    columns = plane_step(planes.reshape(n_tg * slots, 128), stick_pos, cs, potential)
-    applied, image, coef = collect(columns.reshape(n_tg, slots, 128), usable, cs, pack, n_tg, n_pool)
-    rotated, applied = rotate(coef, image, ritz_full, slab_base, applied)
+    planes, pack, usable, cs, col = spread(wave_coef, stick_count, ritz_block, n_tg, n_pool)
+    re, im = lattice(planes.reshape(n_tg * slots, 128), stick_pos, cs)
+    applied, image, coef, ritz = collect(stick_pos, re, im, potential, usable, cs, pack, col, n_tg, n_pool)
+    ritz = ritz.reshape((2 * n_pool,) + ritz_block.shape[1:])
+    rotated, applied = rotate(coef, image, ritz, slab_base, applied)
     return applied.reshape(wave_coef.shape), rotated
 
 

time: 83.5 us -> 75.3 us (0.902)
  between operations: 14.1 us -> 0.65 us
  Pallas kernels: 68.3 us -> 74.3 us
    pallas_call x1, Pallas kernels: 20.2 us -> 37.9 us  [collect(): pl.pallas_call(functools.partial(collect_kernel, n_tg, n_pool), out_shape...]
    pallas_call x1, Pallas kernels: 24.8 us -> 7.95 us  [lattice(): pl.pallas_call(lattice_kernel, out_shape=[jax.ShapeDtypeStruct(size, F32)...]
    pallas_call x1, Pallas kernels: 11.6 us -> 16.6 us  [spread(): pl.pallas_call(functools.partial(spread_kernel, n_tg, n_pool), out_shape=...]
  transfers between devices with their start and end apart: 1 -> 0, of which waited for: 0 -> 0; matrix products, arithmetic and copies ran while one was open for 0% -> 0% of each run, Pallas kernels for 68% -> 0%
where the time goes in v4:
time: 75.3 us; the launch traced here: 74.9 us
  Pallas kernels  74.3 us (99%)
    pallas_call x1, Pallas kernels, collect(): pl.pallas_call(functools.partial(collect_kernel, n_tg, n_pool), out_shape...  37.9 us
    pallas_call x1, Pallas kernels, spread(): pl.pallas_call(functools.partial(spread_kernel, n_tg, n_pool), out_shape=...  16.6 us
    pallas_call x1, Pallas kernels, rotate(): pl.pallas_call(rotate_kernel, grid=(base.shape[2] // COLUMNS,), out_shape...  11.8 us
    pallas_call x1, Pallas kernels, lattice(): pl.pallas_call(lattice_kernel, out_shape=[jax.ShapeDtypeStruct(size, F32)...  7.95 us

profile of v4, /device:TPU:1, one launch (start us, length us, event | category | flops | bytes accessed | tf_op | source)
XLA Modules:
  0.0 74.9 jit_solution(15424942727989628476)
XLA Ops:
  0.6 16.6 %spread.1 = (f32[8,64,128]{2,1,0:T(8,128)}, f32[16,4,8,128]{3,2,1,0:T(8,128)}, f32[64,128]{1,0:T(8,128)}, bf16[4,128,128]{2,1,0:T(8,128)(2,1)}, f32[4,2,4,4096]{3,2,1,0:T(4,128)}) custom-call(f32[2,4,64,128]{3,2,1,0:T(8,128)} %wave_hbm.1, s32[8]{0:T(128)} %count_hbm.1, f32[2,4,4096]{2,1,0:T(4,128)} %ritz_hbm.1), custom_call_target="tpu_custom_call" | custom-call | tf_op jit(solution)/shard_map/spread/pallas_call | solution.py:426
  17.2 7.9 %lattice.1 = (f32[8320,128]{1,0:T(8,128)}, f32[8320,128]{1,0:T(8,128)}) custom-call(s32[512]{0:T(512)} %pos_hbm.3, f32[512,128]{1,0:T(8,128)} %bitcast.4, bf16[4,128,128]{2,1,0:T(8,128)(2,1)} %get-tuple-element.16.cs_hbm), custom_call_target="tpu_custom_call" | custom-call | tf_op jit(solution)/shard_map/lattice/pallas_call | solution.py:133
  25.2 37.9 %collect.1 = (f32[512,128]{1,0:T(8,128)}, f32[16,4,8,128]{3,2,1,0:T(8,128)}, f32[16,4,8,128]{3,2,1,0:T(8,128)}, f32[2,2,4,2,4,4096]{5,4,3,2,1,0:T(4,128)}) custom-call(s32[512]{0:T(512)} %pos_hbm.3, f32[8320,128]{1,0:T(8,128)} %get-tuple-element.17.re_hbm, f32[8320,128]{1,0:T(8,128)} %get-tuple-element.18.im_hbm, f32[16,128,128]{2,1,0:T(8,128)} %pot_hbm.1, ...), custom_call_target="tpu_custom_call" | custom-call | tf_op jit(solution)/shard_map/collect/pallas_call | solution.py:446
  63.1 11.8 %rotate.1 = (bf16[2,512,4096]{2,1,0:T(8,128)(2,1)}, f32[512,128]{1,0:T(8,128)}) custom-call(f32[16,4,8,128]{3,2,1,0:T(8,128)} %get-tuple-element.22.coef_ref, f32[16,4,8,128]{3,2,1,0:T(8,128)} %get-tuple-element.23.image_ref, f32[512,128]{1,0:T(8,128)} %get-tuple-element.24.applied_ref, f32[32,4,4096]{2,1,0:T(4,128)} %bitcast.3, bf16[2,512,4096]{2,1,0:T(8,128)(2,1)} %base_ref.1), custom_call_target="tpu_custom_call" | custom-call | tf_op jit(solution)/shard_map/rotate/pallas_call | solution.py:213

commit v5 on v4

--- a/solution.py
+++ b/solution.py
@@ -66,15 +66,15 @@
     return lax.dot_general(a, b, (((1,), (1,)), ((), ())), preferred_element_type=F32)
 
 
-PITCH = 65
+PITCH = 33
+HALF = 128 * PITCH
 LIMIT = 60 * 2**20
 Y_STEP = 16
-X_STEP = 2
-
-
-def chunk(ref, step):
+
+
+def chunk(ref, pair, step):
     rows = Y_STEP * PITCH
-    return ref.at[pl.ds(pl.multiple_of(step * rows, 8), rows), :]
+    return ref.at[pl.ds(pl.multiple_of(pair * HALF + step * rows, 8), rows), :]
 
 
 def lattice_kernel(pos_hbm, sticks_hbm, cs_hbm, re_hbm, im_hbm,
@@ -103,10 +103,10 @@
             grid_ref[pl.ds(pos_ref[base + k], 1), :] = rows[k:k + 1, :]
 
     def stores(step):
-        return [pltpu.make_async_copy(chunk(src, step), chunk(dst, step), out_sems.at[k, step])
-                for k, (src, dst) in enumerate([(re_ref, re_hbm), (im_ref, im_hbm)])]
-
-    @pl.loop(0, 128 // Y_STEP)
+        return [pltpu.make_async_copy(chunk(src, pair, step), chunk(dst, pair, step), out_sems.at[k, pair, step])
+                for pair in range(2) for k, (src, dst) in enumerate([(re_ref, re_hbm), (im_ref, im_hbm)])]
+
+    @pl.loop(0, 128 // Y_STEP, unroll=8)
     def _(step):
         parts = []
         for k in range(Y_STEP):
@@ -115,9 +115,11 @@
             parts.append(jnp.concatenate([flipped[:half], flipped[half:]], axis=1))
         res = dot(lanes3(jnp.concatenate(parts, axis=0)), ty_ref[...])
         for k in range(Y_STEP):
-            to = pl.ds((step * Y_STEP + k) * PITCH, half)
-            re_ref[to, :] = res[k * half:(k + 1) * half, :128]
-            im_ref[to, :] = res[k * half:(k + 1) * half, 128:]
+            for pair in range(2):
+                to = pl.ds(pair * HALF + (step * Y_STEP + k) * PITCH, 32)
+                at = k * half + pair * 32
+                re_ref[to, :] = res[at:at + 32, :128]
+                im_ref[to, :] = res[at:at + 32, 128:]
         for store in stores(step):
             store.start()
 
@@ -129,7 +131,7 @@
 
 def lattice(sticks, stick_pos, cs):
     hbm = pl.BlockSpec(memory_space=pltpu.HBM)
-    size = (128 * PITCH, 128)
+    size = (2 * HALF, 128)
     return pl.pallas_call(
         lattice_kernel,
         out_shape=[jax.ShapeDtypeStruct(size, F32)] * 2,
@@ -144,37 +146,37 @@
             pltpu.VMEM(size, F32),
             pltpu.VMEM(size, F32),
             pltpu.SemaphoreType.DMA((3,)),
-            pltpu.SemaphoreType.DMA((2, 128 // Y_STEP)),
+            pltpu.SemaphoreType.DMA((2, 2, 128 // Y_STEP)),
         ],
         compiler_params=pltpu.CompilerParams(vmem_limit_bytes=LIMIT),
         name="lattice",
     )(stick_pos, sticks, cs)
 
 
-def x_transforms(pot_ref, ax_ref, bx_ref, re_ref, im_ref):
-    @pl.loop(0, 16, unroll=2)
+def x_transforms(pair, pot_ref, ax_ref, bx_ref, re_ref, im_ref):
+    @pl.loop(0, 16, unroll=16)
     def _(z):
         pot = pot_ref[z]
-        wide = jnp.concatenate([pot] * X_STEP, axis=1)
-        wide = jnp.concatenate([wide, wide], axis=0)
-        for group in range(4 // X_STEP):
-            at = [pl.ds((group * X_STEP + k) * 16 + z, 128, PITCH) for k in range(X_STEP)]
-            data = jnp.concatenate(
-                [jnp.concatenate([re_ref[a, :], im_ref[a, :]], axis=0) for a in at], axis=1)
-            field = dot(ax_ref[...], rows3(data))
-            back = dot(bx_ref[...], rows3(field * wide))
-            for k in range(X_STEP):
-                re_ref[at[k], :] = back[:128, k * 128:(k + 1) * 128]
-                im_ref[at[k], :] = back[128:, k * 128:(k + 1) * 128]
+        wide = jnp.concatenate([pot] * 2, axis=1)
+        wide = jnp.concatenate([wide] * 2, axis=0)
+        at = [pl.ds(pair * HALF + k * 16 + z, 128, PITCH) for k in range(2)]
+        data = jnp.concatenate(
+            [jnp.concatenate([re_ref[a, :], im_ref[a, :]], axis=0) for a in at], axis=1)
+        field = dot(ax_ref[...], rows3(data))
+        back = dot(bx_ref[...], rows3(field * wide))
+        for k in range(2):
+            re_ref[at[k], :] = back[:128, k * 128:(k + 1) * 128]
+            im_ref[at[k], :] = back[128:, k * 128:(k + 1) * 128]
 
 
 def y_transform_back(bx_ref, re_ref, im_ref, grid_ref):
     half = 64
 
-    @pl.loop(0, 128 // Y_STEP)
+    @pl.loop(0, 128 // Y_STEP, unroll=4)
     def _(step):
         data = jnp.concatenate(
-            [jnp.concatenate([ref[pl.ds((step * Y_STEP + k) * PITCH, half), :] for k in range(Y_STEP)], axis=0)
+            [jnp.concatenate([ref[pl.ds(pair * HALF + (step * Y_STEP + k) * PITCH, 32), :]
+                              for k in range(Y_STEP) for pair in range(2)], axis=0)
              for ref in (re_ref, im_ref)], axis=1)
         res = dot_nt(bx_ref[...], lanes3(data))
         for k in range(Y_STEP):
@@ -183,7 +185,7 @@
                 [res[:128, k * half:(k + 1) * half], res[128:, k * half:(k + 1) * half]], axis=1)
 
 
-COLUMNS = 512
+COLUMNS = 1024
 
 
 def rotate_kernel(coef_ref, image_ref, applied_ref, ritz_ref, base_ref, out_ref, copy_ref, left_ref):
@@ -308,6 +310,11 @@
     table_ref[...] = as_rhs_rows(cs, 1)
     loads[0].wait()
     loads[1].wait()
+    pl.semaphore_wait(barrier, n_tg + 1)
+    rise = remote(ritz_hbm, col_hbm.at[z], send_r.at[0], recv_r.at[0], pool=up)
+    fall = remote(ritz_hbm, col_hbm.at[z], send_r.at[1], recv_r.at[1], pool=down)
+    rise.start()
+    fall.start()
     slot = lax.broadcasted_iota(jnp.int32, (64, 128), 0)
     usable = jnp.where(slot < count_ref[tg], 1.0, 0.0).astype(F32)
     usable_ref[...] = usable
@@ -322,13 +329,8 @@
         sticks_ref[t] = jnp.concatenate(
             [res[band * 64:(band + 1) * 64, part * 128 + t * 16:part * 128 + t * 16 + 16]
              for part in range(2) for band in range(4)], axis=1)
-    pl.semaphore_wait(barrier, n_tg + 1)
     planes = Exchange("tg", n_tg, tg, sticks_ref, planes_ref, send_t, recv_t, own_sem.at[0])
     planes.start()
-    rise = remote(ritz_hbm, col_hbm.at[z], send_r.at[0], recv_r.at[0], pool=up)
-    fall = remote(ritz_hbm, col_hbm.at[z], send_r.at[1], recv_r.at[1], pool=down)
-    rise.start()
-    fall.start()
     pack_rows(flat_ref, pack_ref, n_pool)
     remote(ritz_hbm, col_hbm.at[before], send_r.at[0], recv_r.at[0], pool=up).wait_recv()
     rise_on = remote(col_hbm.at[before, 0], col_hbm.at[before, 0], send_r.at[2], recv_r.at[2], pool=up)
@@ -352,8 +354,10 @@
                    send_t, recv_t, send_p, recv_p, send_c, recv_c, own_sem, load_sem, send_r, recv_r):
     tg, pool = lax.axis_index("tg"), lax.axis_index("pool")
     y, z, core = pool_parts(pool)
-    pairs = [(cs_hbm, cs_ref), (re_hbm, re_ref), (im_hbm, im_ref), (pot_hbm, pot_ref),
-             (usable_hbm, usable_ref), (pos_hbm, pos_ref), (col_hbm, ritz_ref.at[y, core])]
+    halves = [(src.at[pl.ds(pair * HALF, HALF), :], dst.at[pl.ds(pair * HALF, HALF), :])
+              for pair in range(2) for src, dst in ((re_hbm, re_ref), (im_hbm, im_ref))]
+    pairs = [(cs_hbm, cs_ref), (pot_hbm, pot_ref)] + halves + [
+        (usable_hbm, usable_ref), (pos_hbm, pos_ref), (col_hbm, ritz_ref.at[y, core])]
     loads = [pltpu.make_async_copy(src, dst, load_sem.at[k]) for k, (src, dst) in enumerate(pairs)]
     for load in loads:
         load.start()
@@ -373,15 +377,17 @@
     to_core.start()
     coef = Exchange("pool", n_pool, pool, pack_hbm, coef_ref, send_c, recv_c, own_sem.at[2])
     coef.start()
-    for load in loads[1:4]:
-        load.wait()
-    x_transforms(pot_ref, ax_ref, bx_ref, re_ref, im_ref)
+    loads[1].wait()
+    for pair in range(2):
+        loads[2 + 2 * pair].wait()
+        loads[3 + 2 * pair].wait()
+        x_transforms(pair, pot_ref, ax_ref, bx_ref, re_ref, im_ref)
+    y_transform_back(bx_ref, re_ref, im_ref, grid_ref)
     remote(col_hbm, ritz_ref.at[1 - y, core], send_r.at[0], recv_r.at[0], pool=next_y).wait_recv()
     on_core = remote(ritz_ref.at[1 - y, core], ritz_ref.at[1 - y, core], send_r.at[2], recv_r.at[2], pool=next_core)
     on_core.start()
-    y_transform_back(bx_ref, re_ref, im_ref, grid_ref)
-    loads[4].wait()
-    loads[5].wait()
+    loads[6].wait()
+    loads[7].wait()
 
     def gather(peer):
         @pl.loop(0, 8)
@@ -408,7 +414,7 @@
     image = Exchange("pool", n_pool, pool, pack_ref, image_ref, send_p, recv_p, own_sem.at[1])
     image.start()
     coef.wait_recv()
-    loads[6].wait()
+    loads[8].wait()
     remote(col_hbm, ritz_ref.at[y, 1 - core], send_r.at[1], recv_r.at[1], pool=next_core).wait_recv()
     remote(ritz_ref.at[1 - y, core], ritz_ref.at[1 - y, 1 - core], send_r.at[2], recv_r.at[2],
            pool=next_core).wait_recv()
@@ -455,7 +461,7 @@
                         pltpu.VMEM((16384, 128), F32), pltpu.VMEM((n_tg, 64, 128), F32),
                         pltpu.VMEM((n_tg, 64, 128), F32), pltpu.VMEM(pack.shape, F32),
                         dma((n_tg,)), dma((n_tg,)), dma((n_pool,)), dma((n_pool,)), dma((n_pool,)), dma((n_pool,)),
-                        dma((3,)), dma((7,)), dma((3,)), dma((3,))],
+                        dma((3,)), dma((9,)), dma((3,)), dma((3,))],
         compiler_params=pltpu.CompilerParams(collective_id=1, has_side_effects=True, vmem_limit_bytes=LIMIT),
         name="collect",
     )(stick_pos, re, im, pot, usable, cs, pack, col)

time: 75.3 us -> 67.4 us (0.90)
  Pallas kernels: 74.3 us -> 66.6 us
    pallas_call x1, Pallas kernels: 37.9 us -> 32.1 us  [collect(): pl.pallas_call(functools.partial(collect_kernel, n_tg, n_pool), out_shape...]
    pallas_call x1, Pallas kernels: 11.8 us -> 10.5 us  [rotate(): pl.pallas_call(rotate_kernel, grid=(base.shape[2] // COLUMNS,), out_shape...]
where the time goes in v5:
time: 67.4 us; the launch traced here: 67.2 us
  Pallas kernels  66.6 us (99%)
    pallas_call x1, Pallas kernels, collect(): pl.pallas_call(functools.partial(collect_kernel, n_tg, n_pool), out_shape...  32.1 us
    pallas_call x1, Pallas kernels, spread(): pl.pallas_call(functools.partial(spread_kernel, n_tg, n_pool), out_shape=...  16.5 us
    pallas_call x1, Pallas kernels, rotate(): pl.pallas_call(rotate_kernel, grid=(base.shape[2] // COLUMNS,), out_shape...  10.5 us
    pallas_call x1, Pallas kernels, lattice(): pl.pallas_call(lattice_kernel, out_shape=[jax.ShapeDtypeStruct(size, F32)...  7.44 us

profile of v5, /device:TPU:1, one launch (start us, length us, event | category | flops | bytes accessed | tf_op | source)
XLA Modules:
  0.0 67.2 jit_solution(12790116566552544744)
XLA Ops:
  0.6 16.5 %spread.1 = (f32[8,64,128]{2,1,0:T(8,128)}, f32[16,4,8,128]{3,2,1,0:T(8,128)}, f32[64,128]{1,0:T(8,128)}, bf16[4,128,128]{2,1,0:T(8,128)(2,1)}, f32[4,2,4,4096]{3,2,1,0:T(4,128)}) custom-call(f32[2,4,64,128]{3,2,1,0:T(8,128)} %wave_hbm.1, s32[8]{0:T(128)} %count_hbm.1, f32[2,4,4096]{2,1,0:T(4,128)} %ritz_hbm.1), custom_call_target="tpu_custom_call" | custom-call | tf_op jit(solution)/shard_map/spread/pallas_call | solution.py:432
  17.2 7.4 %lattice.1 = (f32[8448,128]{1,0:T(8,128)}, f32[8448,128]{1,0:T(8,128)}) custom-call(s32[512]{0:T(512)} %pos_hbm.3, f32[512,128]{1,0:T(8,128)} %bitcast.4, bf16[4,128,128]{2,1,0:T(8,128)(2,1)} %get-tuple-element.16.cs_hbm), custom_call_target="tpu_custom_call" | custom-call | tf_op jit(solution)/shard_map/lattice/pallas_call | solution.py:135
  24.6 32.1 %collect.1 = (f32[512,128]{1,0:T(8,128)}, f32[16,4,8,128]{3,2,1,0:T(8,128)}, f32[16,4,8,128]{3,2,1,0:T(8,128)}, f32[2,2,4,2,4,4096]{5,4,3,2,1,0:T(4,128)}) custom-call(s32[512]{0:T(512)} %pos_hbm.3, f32[8448,128]{1,0:T(8,128)} %get-tuple-element.17.re_hbm, f32[8448,128]{1,0:T(8,128)} %get-tuple-element.18.im_hbm, f32[16,128,128]{2,1,0:T(8,128)} %pot_hbm.1, ...), custom_call_target="tpu_custom_call" | custom-call | tf_op jit(solution)/shard_map/collect/pallas_call | solution.py:452
  56.7 10.5 %rotate.1 = (bf16[2,512,4096]{2,1,0:T(8,128)(2,1)}, f32[512,128]{1,0:T(8,128)}) custom-call(f32[16,4,8,128]{3,2,1,0:T(8,128)} %get-tuple-element.22.coef_ref, f32[16,4,8,128]{3,2,1,0:T(8,128)} %get-tuple-element.23.image_ref, f32[512,128]{1,0:T(8,128)} %get-tuple-element.24.applied_ref, f32[32,4,4096]{2,1,0:T(4,128)} %bitcast.3, bf16[2,512,4096]{2,1,0:T(8,128)(2,1)} %base_ref.1), custom_call_target="tpu_custom_call" | custom-call | tf_op jit(solution)/shard_map/rotate/pallas_call | solution.py:215

commit v6 on v5

--- a/solution.py
+++ b/solution.py
@@ -186,40 +186,81 @@
 
 
 COLUMNS = 1024
-
-
-def rotate_kernel(coef_ref, image_ref, applied_ref, ritz_ref, base_ref, out_ref, copy_ref, left_ref):
-    @pl.when(pl.program_id(0) == 0)
-    def _():
-        copy_ref[...] = applied_ref[...]
+DEPTH = 2
+
+
+def rotate_kernel(coef_hbm, image_hbm, applied_hbm, ritz_hbm, base_hbm, out_hbm, copy_hbm,
+                  coef_ref, image_ref, ritz_ref, slab_ref, left_ref, small_sem, ritz_sem, in_sem, out_sem):
+    steps = slab_ref.shape[2] // COLUMNS
+
+    def at(step):
+        return pl.ds(pl.multiple_of(step * COLUMNS, COLUMNS), COLUMNS)
+
+    def load_ritz(step):
+        return pltpu.make_async_copy(ritz_hbm.at[:, :, at(step)], ritz_ref.at[:, :, at(step)], ritz_sem.at[step])
+
+    def load(step):
+        return pltpu.make_async_copy(base_hbm.at[:, :, at(step)], slab_ref.at[:, :, at(step)], in_sem.at[step])
+
+    def store(step):
+        return pltpu.make_async_copy(slab_ref.at[:, :, at(step)], out_hbm.at[:, :, at(step)], out_sem.at[step])
+
+    pairs = [(coef_hbm, coef_ref), (image_hbm, image_ref), (applied_hbm, copy_hbm)]
+    small = [pltpu.make_async_copy(src, dst, small_sem.at[k]) for k, (src, dst) in enumerate(pairs)]
+    small[0].start()
+    small[1].start()
+    for step in range(DEPTH):
+        load_ritz(step).start()
+        load(step).start()
+    small[2].start()
+    small[0].wait()
+    small[1].wait()
+    for part in range(2):
+        for slot in range(4):
+            rows = jnp.concatenate(
+                [ref[(y * 4 + z) * 2 + core, slot, part * 4:part * 4 + 4, :]
+                 for y in range(2) for core in range(2) for z in range(4) for ref in (coef_ref, image_ref)],
+                axis=0).T
+            high, low = split(rows)
+            to = (part * 4 + slot) * 128
+            left_ref[to:to + 128, :] = jnp.concatenate([high, low, high, low], axis=1)
+
+    @pl.loop(0, steps)
+    def _(step):
+        load_ritz(step).wait()
+        high, low = split(jnp.concatenate([ritz_ref[k, :, at(step)] for k in range(ritz_ref.shape[0])], axis=0))
+        right = jnp.concatenate([high, high, low, low], axis=0)
+        load(step).wait()
+
+        @pl.when(step + DEPTH < steps)
+        def _():
+            load_ritz(step + DEPTH).start()
+            load(step + DEPTH).start()
+
         for part in range(2):
-            for slot in range(4):
-                rows = jnp.concatenate(
-                    [ref[(y * 4 + z) * 2 + core, slot, part * 4:part * 4 + 4, :]
-                     for y in range(2) for core in range(2) for z in range(4) for ref in (coef_ref, image_ref)],
-                    axis=0).T
-                high, low = split(rows)
-                at = (part * 4 + slot) * 128
-                left_ref[at:at + 128, :] = jnp.concatenate([high, low, high, low], axis=1)
-
-    high, low = split(jnp.concatenate([ritz_ref[k] for k in range(ritz_ref.shape[0])], axis=0))
-    right = jnp.concatenate([high, high, low, low], axis=0)
-    for part in range(2):
-        out_ref[part] = (base_ref[part].astype(F32)
-                         + dot(left_ref[part * 512:(part + 1) * 512, :], right)).astype(BF16)
+            res = dot(left_ref[part * 512:(part + 1) * 512, :], right)
+            slab_ref[part, :, at(step)] = (slab_ref[part, :, at(step)].astype(F32) + res).astype(BF16)
+        store(step).start()
+
+    @pl.loop(0, steps)
+    def _(step):
+        store(step).wait()
+
+    small[2].wait()
 
 
 def rotate(coef, image, ritz, base, applied):
-    once = lambda a: pl.BlockSpec(a.shape, lambda j: (0,) * a.ndim)
-    slab = pl.BlockSpec((2, base.shape[1], COLUMNS), lambda j: (0, 0, j))
+    hbm = pl.BlockSpec(memory_space=pltpu.HBM)
+    dma = pltpu.SemaphoreType.DMA
+    steps = base.shape[2] // COLUMNS
     return pl.pallas_call(
         rotate_kernel,
-        grid=(base.shape[2] // COLUMNS,),
         out_shape=[jax.ShapeDtypeStruct(base.shape, BF16), jax.ShapeDtypeStruct(applied.shape, F32)],
-        in_specs=[once(coef), once(image), once(applied),
-                  pl.BlockSpec(ritz.shape[:2] + (COLUMNS,), lambda j: (0, 0, j)), slab],
-        out_specs=[slab, once(applied)],
-        scratch_shapes=[pltpu.VMEM((1024, 512), BF16)],
+        in_specs=[hbm] * 5,
+        out_specs=[hbm] * 2,
+        scratch_shapes=[pltpu.VMEM(coef.shape, F32), pltpu.VMEM(image.shape, F32), pltpu.VMEM(ritz.shape, F32),
+                        pltpu.VMEM(base.shape, BF16), pltpu.VMEM((1024, 512), BF16),
+                        dma((3,)), dma((steps,)), dma((steps,)), dma((steps,))],
         compiler_params=pltpu.CompilerParams(vmem_limit_bytes=LIMIT),
         name="rotate",
     )(coef, image, applied, ritz, base)
@@ -368,6 +409,10 @@
     ax_ref[...] = as_lhs(cs, 1) * (1.0 / 128.0 ** 3)
     bx_ref[...] = as_lhs(cs, -1)
     table_ref[...] = as_rhs_rows(cs, -1)
+    loads[1].wait()
+    loads[2].wait()
+    loads[3].wait()
+    x_transforms(0, pot_ref, ax_ref, bx_ref, re_ref, im_ref)
     pl.semaphore_wait(barrier, n_tg + n_pool - 2)
     next_core = pool_index(y, z, 1 - core)
     next_y = pool_index(1 - y, z, core)
@@ -377,11 +422,9 @@
     to_core.start()
     coef = Exchange("pool", n_pool, pool, pack_hbm, coef_ref, send_c, recv_c, own_sem.at[2])
     coef.start()
-    loads[1].wait()
-    for pair in range(2):
-        loads[2 + 2 * pair].wait()
-        loads[3 + 2 * pair].wait()
-        x_transforms(pair, pot_ref, ax_ref, bx_ref, re_ref, im_ref)
+    loads[4].wait()
+    loads[5].wait()
+    x_transforms(1, pot_ref, ax_ref, bx_ref, re_ref, im_ref)
     y_transform_back(bx_ref, re_ref, im_ref, grid_ref)
     remote(col_hbm, ritz_ref.at[1 - y, core], send_r.at[0], recv_r.at[0], pool=next_y).wait_recv()
     on_core = remote(ritz_ref.at[1 - y, core], ritz_ref.at[1 - y, core], send_r.at[2], recv_r.at[2], pool=next_core)

time: 67.4 us -> 69.9 us (1.037)
  Pallas kernels: 66.6 us -> 68.9 us
    pallas_call x1, Pallas kernels: 32.1 us -> 35.7 us  [collect(): pl.pallas_call(functools.partial(collect_kernel, n_tg, n_pool), out_shape...]
    pallas_call x1, Pallas kernels: 10.5 us -> 9.22 us  [rotate(): pl.pallas_call(rotate_kernel, out_shape=[jax.ShapeDtypeStruct(base.shape,...]
where the time goes in v6:
time: 69.9 us; the launch traced here: 69.7 us
  Pallas kernels  68.9 us (99%)
  between operations  0.81 us (1%)
    pallas_call x1, Pallas kernels, collect(): pl.pallas_call(functools.partial(collect_kernel, n_tg, n_pool), out_shape...  35.7 us
    pallas_call x1, Pallas kernels, spread(): pl.pallas_call(functools.partial(spread_kernel, n_tg, n_pool), out_shape=...  16.5 us
    pallas_call x1, Pallas kernels, rotate(): pl.pallas_call(rotate_kernel, out_shape=[jax.ShapeDtypeStruct(base.shape,...  9.22 us
    pallas_call x1, Pallas kernels, lattice(): pl.pallas_call(lattice_kernel, out_shape=[jax.ShapeDtypeStruct(size, F32)...  7.44 us

profile of v6, /device:TPU:1, one launch (start us, length us, event | category | flops | bytes accessed | tf_op | source)
XLA Modules:
  0.0 69.7 jit_solution(1345389909828176731)
XLA Ops:
  0.6 16.5 %spread.1 = (f32[8,64,128]{2,1,0:T(8,128)}, f32[16,4,8,128]{3,2,1,0:T(8,128)}, f32[64,128]{1,0:T(8,128)}, bf16[4,128,128]{2,1,0:T(8,128)(2,1)}, f32[4,2,4,4096]{3,2,1,0:T(4,128)}) custom-call(f32[2,4,64,128]{3,2,1,0:T(8,128)} %wave_hbm.1, s32[8]{0:T(128)} %count_hbm.1, f32[2,4,4096]{2,1,0:T(4,128)} %ritz_hbm.1), custom_call_target="tpu_custom_call" | custom-call | tf_op jit(solution)/shard_map/spread/pallas_call | solution.py:475
  17.2 7.4 %lattice.1 = (f32[8448,128]{1,0:T(8,128)}, f32[8448,128]{1,0:T(8,128)}) custom-call(s32[512]{0:T(512)} %pos_hbm.3, f32[512,128]{1,0:T(8,128)} %bitcast.4, bf16[4,128,128]{2,1,0:T(8,128)(2,1)} %get-tuple-element.16.cs_hbm), custom_call_target="tpu_custom_call" | custom-call | tf_op jit(solution)/shard_map/lattice/pallas_call | solution.py:135
  24.6 35.7 %collect.1 = (f32[512,128]{1,0:T(8,128)}, f32[16,4,8,128]{3,2,1,0:T(8,128)}, f32[16,4,8,128]{3,2,1,0:T(8,128)}, f32[2,2,4,2,4,4096]{5,4,3,2,1,0:T(4,128)}) custom-call(s32[512]{0:T(512)} %pos_hbm.3, f32[8448,128]{1,0:T(8,128)} %get-tuple-element.17.re_hbm, f32[8448,128]{1,0:T(8,128)} %get-tuple-element.18.im_hbm, f32[16,128,128]{2,1,0:T(8,128)} %pot_hbm.1, ...), custom_call_target="tpu_custom_call" | custom-call | tf_op jit(solution)/shard_map/collect/pallas_call | solution.py:495
  60.3 9.2 %rotate.1 = (bf16[2,512,4096]{2,1,0:T(8,128)(2,1)}, f32[512,128]{1,0:T(8,128)}) custom-call(f32[16,4,8,128]{3,2,1,0:T(8,128)} %get-tuple-element.22.coef_hbm, f32[16,4,8,128]{3,2,1,0:T(8,128)} %get-tuple-element.23.image_hbm, f32[512,128]{1,0:T(8,128)} %get-tuple-element.24.applied_hbm, f32[32,4,4096]{2,1,0:T(4,128)} %bitcast.3, bf16[2,512,4096]{2,1,0:T(8,128)(2,1)} %base_hbm.1), custom_call_target="tpu_custom_call" | custom-call | tf_op jit(solution)/shard_map/rotate/pallas_call | solution.py:256

commit v7 on v6

--- a/solution.py
+++ b/solution.py
@@ -336,7 +336,7 @@
                   send_r, recv_r):
     tg, pool = lax.axis_index("tg"), lax.axis_index("pool")
     y, z, core = pool_parts(pool)
-    after, before, across = lax.rem(z + 1, 4), lax.rem(z + 3, 4), lax.rem(z + 2, 4)
+    after, before = lax.rem(z + 1, 4), lax.rem(z + 3, 4)
     up, down = pool_index(y, after, core), pool_index(y, before, core)
     pairs = [(count_hbm, count_ref), (wave_hbm, wave_ref), (ritz_hbm, col_hbm.at[z])]
     loads = [pltpu.make_async_copy(src, dst, load_sem.at[k]) for k, (src, dst) in enumerate(pairs)]
@@ -373,19 +373,13 @@
     planes = Exchange("tg", n_tg, tg, sticks_ref, planes_ref, send_t, recv_t, own_sem.at[0])
     planes.start()
     pack_rows(flat_ref, pack_ref, n_pool)
+    planes.wait_recv()
     remote(ritz_hbm, col_hbm.at[before], send_r.at[0], recv_r.at[0], pool=up).wait_recv()
-    rise_on = remote(col_hbm.at[before, 0], col_hbm.at[before, 0], send_r.at[2], recv_r.at[2], pool=up)
-    rise_on.start()
     remote(ritz_hbm, col_hbm.at[after], send_r.at[1], recv_r.at[1], pool=down).wait_recv()
-    fall_on = remote(col_hbm.at[after, 1], col_hbm.at[after, 1], send_r.at[3], recv_r.at[3], pool=down)
-    fall_on.start()
-    planes.wait_recv()
-    remote(col_hbm.at[before, 0], col_hbm.at[across, 0], send_r.at[2], recv_r.at[2], pool=up).wait_recv()
-    remote(col_hbm.at[after, 1], col_hbm.at[across, 1], send_r.at[3], recv_r.at[3], pool=down).wait_recv()
     loads[2].wait()
     planes.wait_send()
-    for copy in (rise, fall, rise_on, fall_on):
-        copy.wait_send()
+    rise.wait_send()
+    fall.wait_send()
 
 
 def collect_kernel(n_tg, n_pool, pos_hbm, re_hbm, im_hbm, pot_hbm, usable_hbm, cs_hbm, pack_hbm, col_hbm,
@@ -395,10 +389,14 @@
                    send_t, recv_t, send_p, recv_p, send_c, recv_c, own_sem, load_sem, send_r, recv_r):
     tg, pool = lax.axis_index("tg"), lax.axis_index("pool")
     y, z, core = pool_parts(pool)
+    after, before, across = lax.rem(z + 1, 4), lax.rem(z + 3, 4), lax.rem(z + 2, 4)
+    up, down = pool_index(y, after, core), pool_index(y, before, core)
+    next_core, next_y = pool_index(y, z, 1 - core), pool_index(1 - y, z, core)
+    own, other = ritz_ref.at[y, core], ritz_ref.at[1 - y, core]
     halves = [(src.at[pl.ds(pair * HALF, HALF), :], dst.at[pl.ds(pair * HALF, HALF), :])
               for pair in range(2) for src, dst in ((re_hbm, re_ref), (im_hbm, im_ref))]
     pairs = [(cs_hbm, cs_ref), (pot_hbm, pot_ref)] + halves + [
-        (usable_hbm, usable_ref), (pos_hbm, pos_ref), (col_hbm, ritz_ref.at[y, core])]
+        (usable_hbm, usable_ref), (pos_hbm, pos_ref)] + [(col_hbm.at[k], own.at[k]) for k in (z, before, after)]
     loads = [pltpu.make_async_copy(src, dst, load_sem.at[k]) for k, (src, dst) in enumerate(pairs)]
     for load in loads:
         load.start()
@@ -409,26 +407,47 @@
     ax_ref[...] = as_lhs(cs, 1) * (1.0 / 128.0 ** 3)
     bx_ref[...] = as_lhs(cs, -1)
     table_ref[...] = as_rhs_rows(cs, -1)
-    loads[1].wait()
-    loads[2].wait()
-    loads[3].wait()
-    x_transforms(0, pot_ref, ax_ref, bx_ref, re_ref, im_ref)
     pl.semaphore_wait(barrier, n_tg + n_pool - 2)
-    next_core = pool_index(y, z, 1 - core)
-    next_y = pool_index(1 - y, z, core)
-    to_y = remote(col_hbm, ritz_ref.at[y, core], send_r.at[0], recv_r.at[0], pool=next_y)
-    to_core = remote(col_hbm, ritz_ref.at[y, core], send_r.at[1], recv_r.at[1], pool=next_core)
-    to_y.start()
-    to_core.start()
+
+    def ritz(k, src, dst, peer):
+        return remote(src, dst, send_r.at[k], recv_r.at[k], pool=peer)
+
+    sent = [ritz(0, col_hbm.at[z], own.at[z], next_y),
+            ritz(1, col_hbm.at[before, 0], own.at[before, 0], up),
+            ritz(2, col_hbm.at[after, 1], own.at[after, 1], down)]
+    for copy in sent:
+        copy.start()
     coef = Exchange("pool", n_pool, pool, pack_hbm, coef_ref, send_c, recv_c, own_sem.at[2])
     coef.start()
+    for load in loads[1:4]:
+        load.wait()
+    x_transforms(0, pot_ref, ax_ref, bx_ref, re_ref, im_ref)
+    for load in loads[8:11]:
+        load.wait()
+    ritz(0, other.at[z], other.at[z], next_y).wait_recv()
+    ritz(1, own.at[across, 0], own.at[across, 0], up).wait_recv()
+    ritz(2, own.at[across, 1], own.at[across, 1], down).wait_recv()
+    stage = [ritz(3, other.at[z], other.at[z], up), ritz(4, other.at[z], other.at[z], down),
+             ritz(5, own, own, next_core)]
+    for copy in stage:
+        copy.start()
+    sent += stage
     loads[4].wait()
     loads[5].wait()
     x_transforms(1, pot_ref, ax_ref, bx_ref, re_ref, im_ref)
+    ritz(3, other.at[before], other.at[before], up).wait_recv()
+    ritz(4, other.at[after], other.at[after], down).wait_recv()
+    stage = [ritz(6, other.at[before, 0], other.at[before, 0], up),
+             ritz(7, other.at[after, 1], other.at[after, 1], down)]
+    for copy in stage:
+        copy.start()
+    sent += stage
     y_transform_back(bx_ref, re_ref, im_ref, grid_ref)
-    remote(col_hbm, ritz_ref.at[1 - y, core], send_r.at[0], recv_r.at[0], pool=next_y).wait_recv()
-    on_core = remote(ritz_ref.at[1 - y, core], ritz_ref.at[1 - y, core], send_r.at[2], recv_r.at[2], pool=next_core)
-    on_core.start()
+    ritz(6, other.at[across, 0], other.at[across, 0], up).wait_recv()
+    ritz(7, other.at[across, 1], other.at[across, 1], down).wait_recv()
+    stage = [ritz(8, other, other, next_core)]
+    stage[0].start()
+    sent += stage
     loads[6].wait()
     loads[7].wait()
 
@@ -457,14 +476,12 @@
     image = Exchange("pool", n_pool, pool, pack_ref, image_ref, send_p, recv_p, own_sem.at[1])
     image.start()
     coef.wait_recv()
-    loads[8].wait()
-    remote(col_hbm, ritz_ref.at[y, 1 - core], send_r.at[1], recv_r.at[1], pool=next_core).wait_recv()
-    remote(ritz_ref.at[1 - y, core], ritz_ref.at[1 - y, 1 - core], send_r.at[2], recv_r.at[2],
-           pool=next_core).wait_recv()
+    ritz(5, own, ritz_ref.at[y, 1 - core], next_core).wait_recv()
+    ritz(8, other, ritz_ref.at[1 - y, 1 - core], next_core).wait_recv()
     image.wait_recv()
     for exchange in (back, coef, image):
         exchange.wait_send()
-    for copy in (to_y, to_core, on_core):
+    for copy in sent:
         copy.wait_send()
 
 
@@ -482,7 +499,7 @@
         scratch_shapes=[pltpu.VMEM(wave.shape, F32), pltpu.SMEM(count.shape, jnp.int32),
                         pltpu.VMEM((768, 256), BF16), pltpu.VMEM((512, 128), F32),
                         pltpu.VMEM((n_tg, 64, 128), F32), dma((n_tg,)), dma((n_tg,)), dma((1,)), dma((3,)),
-                        dma((4,)), dma((4,))],
+                        dma((2,)), dma((2,))],
         compiler_params=pltpu.CompilerParams(collective_id=0, has_side_effects=True, vmem_limit_bytes=LIMIT),
         name="spread",
     )(wave, count, ritz)
@@ -504,7 +521,7 @@
                         pltpu.VMEM((16384, 128), F32), pltpu.VMEM((n_tg, 64, 128), F32),
                         pltpu.VMEM((n_tg, 64, 128), F32), pltpu.VMEM(pack.shape, F32),
                         dma((n_tg,)), dma((n_tg,)), dma((n_pool,)), dma((n_pool,)), dma((n_pool,)), dma((n_pool,)),
-                        dma((3,)), dma((9,)), dma((3,)), dma((3,))],
+                        dma((3,)), dma((11,)), dma((9,)), dma((9,))],
         compiler_params=pltpu.CompilerParams(collective_id=1, has_side_effects=True, vmem_limit_bytes=LIMIT),
         name="collect",
     )(stick_pos, re, im, pot, usable, cs, pack, col)

time: 69.9 us -> 69.9 us (level)
    pallas_call x1, Pallas kernels: 35.7 us -> 37.8 us  [collect(): pl.pallas_call(functools.partial(collect_kernel, n_tg, n_pool), out_shape...]
    pallas_call x1, Pallas kernels: 16.5 us -> 14.4 us  [spread(): pl.pallas_call(functools.partial(spread_kernel, n_tg, n_pool), out_shape=...]
where the time goes in v7:
time: 69.9 us; the launch traced here: 69.7 us
  Pallas kernels  68.9 us (99%)
  between operations  0.81 us (1%)
    pallas_call x1, Pallas kernels, collect(): pl.pallas_call(functools.partial(collect_kernel, n_tg, n_pool), out_shape...  37.8 us
    pallas_call x1, Pallas kernels, spread(): pl.pallas_call(functools.partial(spread_kernel, n_tg, n_pool), out_shape=...  14.4 us
    pallas_call x1, Pallas kernels, rotate(): pl.pallas_call(rotate_kernel, out_shape=[jax.ShapeDtypeStruct(base.shape,...  9.22 us
    pallas_call x1, Pallas kernels, lattice(): pl.pallas_call(lattice_kernel, out_shape=[jax.ShapeDtypeStruct(size, F32)...  7.44 us

profile of v7, /device:TPU:1, one launch (start us, length us, event | category | flops | bytes accessed | tf_op | source)
XLA Modules:
  0.0 69.7 jit_solution(9886675484601957067)
XLA Ops:
  0.6 14.4 %spread.1 = (f32[8,64,128]{2,1,0:T(8,128)}, f32[16,4,8,128]{3,2,1,0:T(8,128)}, f32[64,128]{1,0:T(8,128)}, bf16[4,128,128]{2,1,0:T(8,128)(2,1)}, f32[4,2,4,4096]{3,2,1,0:T(4,128)}) custom-call(f32[2,4,64,128]{3,2,1,0:T(8,128)} %wave_hbm.1, s32[8]{0:T(128)} %count_hbm.1, f32[2,4,4096]{2,1,0:T(4,128)} %ritz_hbm.1), custom_call_target="tpu_custom_call" | custom-call | tf_op jit(solution)/shard_map/spread/pallas_call | solution.py:492
  15.0 7.4 %lattice.1 = (f32[8448,128]{1,0:T(8,128)}, f32[8448,128]{1,0:T(8,128)}) custom-call(s32[512]{0:T(512)} %pos_hbm.3, f32[512,128]{1,0:T(8,128)} %bitcast.4, bf16[4,128,128]{2,1,0:T(8,128)(2,1)} %get-tuple-element.16.cs_hbm), custom_call_target="tpu_custom_call" | custom-call | tf_op jit(solution)/shard_map/lattice/pallas_call | solution.py:135
  22.5 37.8 %collect.1 = (f32[512,128]{1,0:T(8,128)}, f32[16,4,8,128]{3,2,1,0:T(8,128)}, f32[16,4,8,128]{3,2,1,0:T(8,128)}, f32[2,2,4,2,4,4096]{5,4,3,2,1,0:T(4,128)}) custom-call(s32[512]{0:T(512)} %pos_hbm.3, f32[8448,128]{1,0:T(8,128)} %get-tuple-element.17.re_hbm, f32[8448,128]{1,0:T(8,128)} %get-tuple-element.18.im_hbm, f32[16,128,128]{2,1,0:T(8,128)} %pot_hbm.1, ...), custom_call_target="tpu_custom_call" | custom-call | tf_op jit(solution)/shard_map/collect/pallas_call | solution.py:512
  60.3 9.2 %rotate.1 = (bf16[2,512,4096]{2,1,0:T(8,128)(2,1)}, f32[512,128]{1,0:T(8,128)}) custom-call(f32[16,4,8,128]{3,2,1,0:T(8,128)} %get-tuple-element.22.coef_hbm, f32[16,4,8,128]{3,2,1,0:T(8,128)} %get-tuple-element.23.image_hbm, f32[512,128]{1,0:T(8,128)} %get-tuple-element.24.applied_hbm, f32[32,4,4096]{2,1,0:T(4,128)} %bitcast.3, bf16[2,512,4096]{2,1,0:T(8,128)(2,1)} %base_hbm.1), custom_call_target="tpu_custom_call" | custom-call | tf_op jit(solution)/shard_map/rotate/pallas_call | solution.py:256

commit v8 on v7

--- a/solution.py
+++ b/solution.py
@@ -398,7 +398,8 @@
     pairs = [(cs_hbm, cs_ref), (pot_hbm, pot_ref)] + halves + [
         (usable_hbm, usable_ref), (pos_hbm, pos_ref)] + [(col_hbm.at[k], own.at[k]) for k in (z, before, after)]
     loads = [pltpu.make_async_copy(src, dst, load_sem.at[k]) for k, (src, dst) in enumerate(pairs)]
-    for load in loads:
+    later = loads[4:6]
+    for load in loads[:4] + loads[6:]:
         load.start()
     barrier = greet("tg", n_tg, tg)
     greet("pool", n_pool, pool)
@@ -412,42 +413,35 @@
     def ritz(k, src, dst, peer):
         return remote(src, dst, send_r.at[k], recv_r.at[k], pool=peer)
 
-    sent = [ritz(0, col_hbm.at[z], own.at[z], next_y),
-            ritz(1, col_hbm.at[before, 0], own.at[before, 0], up),
-            ritz(2, col_hbm.at[after, 1], own.at[after, 1], down)]
+    sent = [ritz(0, col_hbm.at[before, 0], own.at[before, 0], up),
+            ritz(1, col_hbm.at[after, 1], own.at[after, 1], down)]
+    for k, block in enumerate((z, before, after)):
+        sent += [ritz(2 + k, col_hbm.at[block], own.at[block], next_y),
+                 ritz(6 + k, col_hbm.at[block], own.at[block], next_core)]
     for copy in sent:
         copy.start()
-    coef = Exchange("pool", n_pool, pool, pack_hbm, coef_ref, send_c, recv_c, own_sem.at[2])
-    coef.start()
     for load in loads[1:4]:
         load.wait()
+    for load in later:
+        load.start()
     x_transforms(0, pot_ref, ax_ref, bx_ref, re_ref, im_ref)
-    for load in loads[8:11]:
-        load.wait()
-    ritz(0, other.at[z], other.at[z], next_y).wait_recv()
-    ritz(1, own.at[across, 0], own.at[across, 0], up).wait_recv()
-    ritz(2, own.at[across, 1], own.at[across, 1], down).wait_recv()
-    stage = [ritz(3, other.at[z], other.at[z], up), ritz(4, other.at[z], other.at[z], down),
-             ritz(5, own, own, next_core)]
+    ritz(0, own.at[across, 0], own.at[across, 0], up).wait_recv()
+    ritz(1, own.at[across, 1], own.at[across, 1], down).wait_recv()
+    stage = [ritz(5, own.at[across], own.at[across], next_y), ritz(9, own.at[across], own.at[across], next_core)]
     for copy in stage:
         copy.start()
     sent += stage
-    loads[4].wait()
-    loads[5].wait()
+    for load in later:
+        load.wait()
     x_transforms(1, pot_ref, ax_ref, bx_ref, re_ref, im_ref)
-    ritz(3, other.at[before], other.at[before], up).wait_recv()
-    ritz(4, other.at[after], other.at[after], down).wait_recv()
-    stage = [ritz(6, other.at[before, 0], other.at[before, 0], up),
-             ritz(7, other.at[after, 1], other.at[after, 1], down)]
-    for copy in stage:
-        copy.start()
-    sent += stage
     y_transform_back(bx_ref, re_ref, im_ref, grid_ref)
-    ritz(6, other.at[across, 0], other.at[across, 0], up).wait_recv()
-    ritz(7, other.at[across, 1], other.at[across, 1], down).wait_recv()
-    stage = [ritz(8, other, other, next_core)]
-    stage[0].start()
-    sent += stage
+    coef = Exchange("pool", n_pool, pool, pack_hbm, coef_ref, send_c, recv_c, own_sem.at[2])
+    coef.start()
+    for k, block in enumerate((z, before, after, across)):
+        ritz(2 + k, other.at[block], other.at[block], next_y).wait_recv()
+    on_core = ritz(10, other, other, next_core)
+    on_core.start()
+    sent.append(on_core)
     loads[6].wait()
     loads[7].wait()
 
@@ -476,8 +470,12 @@
     image = Exchange("pool", n_pool, pool, pack_ref, image_ref, send_p, recv_p, own_sem.at[1])
     image.start()
     coef.wait_recv()
-    ritz(5, own, ritz_ref.at[y, 1 - core], next_core).wait_recv()
-    ritz(8, other, ritz_ref.at[1 - y, 1 - core], next_core).wait_recv()
+    for load in loads[8:]:
+        load.wait()
+    theirs = ritz_ref.at[y, 1 - core]
+    for k, block in enumerate((z, before, after, across)):
+        ritz(6 + k, own.at[block], theirs.at[block], next_core).wait_recv()
+    ritz(10, other, ritz_ref.at[1 - y, 1 - core], next_core).wait_recv()
     image.wait_recv()
     for exchange in (back, coef, image):
         exchange.wait_send()
@@ -521,7 +519,7 @@
                         pltpu.VMEM((16384, 128), F32), pltpu.VMEM((n_tg, 64, 128), F32),
                         pltpu.VMEM((n_tg, 64, 128), F32), pltpu.VMEM(pack.shape, F32),
                         dma((n_tg,)), dma((n_tg,)), dma((n_pool,)), dma((n_pool,)), dma((n_pool,)), dma((n_pool,)),
-                        dma((3,)), dma((11,)), dma((9,)), dma((9,))],
+                        dma((3,)), dma((11,)), dma((11,)), dma((11,))],
         compiler_params=pltpu.CompilerParams(collective_id=1, has_side_effects=True, vmem_limit_bytes=LIMIT),
         name="collect",
     )(stick_pos, re, im, pot, usable, cs, pack, col)

time: 69.9 us -> 63.9 us (0.914)
  Pallas kernels: 68.9 us -> 62.9 us
    pallas_call x1, Pallas kernels: 37.8 us -> 31.9 us  [collect(): pl.pallas_call(functools.partial(collect_kernel, n_tg, n_pool), out_shape...]
where the time goes in v8:
time: 63.9 us; the launch traced here: 63.7 us
  Pallas kernels  62.9 us (98%)
  between operations  0.81 us (1%)
    pallas_call x1, Pallas kernels, collect(): pl.pallas_call(functools.partial(collect_kernel, n_tg, n_pool), out_shape...  31.9 us
    pallas_call x1, Pallas kernels, spread(): pl.pallas_call(functools.partial(spread_kernel, n_tg, n_pool), out_shape=...  14.4 us
    pallas_call x1, Pallas kernels, rotate(): pl.pallas_call(rotate_kernel, out_shape=[jax.ShapeDtypeStruct(base.shape,...  9.22 us
    pallas_call x1, Pallas kernels, lattice(): pl.pallas_call(lattice_kernel, out_shape=[jax.ShapeDtypeStruct(size, F32)...  7.44 us

profile of v8, /device:TPU:1, one launch (start us, length us, event | category | flops | bytes accessed | tf_op | source)
XLA Modules:
  0.0 63.7 jit_solution(9668131774613743068)
XLA Ops:
  0.6 14.4 %spread.1 = (f32[8,64,128]{2,1,0:T(8,128)}, f32[16,4,8,128]{3,2,1,0:T(8,128)}, f32[64,128]{1,0:T(8,128)}, bf16[4,128,128]{2,1,0:T(8,128)(2,1)}, f32[4,2,4,4096]{3,2,1,0:T(4,128)}) custom-call(f32[2,4,64,128]{3,2,1,0:T(8,128)} %wave_hbm.1, s32[8]{0:T(128)} %count_hbm.1, f32[2,4,4096]{2,1,0:T(4,128)} %ritz_hbm.1), custom_call_target="tpu_custom_call" | custom-call | tf_op jit(solution)/shard_map/spread/pallas_call | solution.py:490
  15.0 7.4 %lattice.1 = (f32[8448,128]{1,0:T(8,128)}, f32[8448,128]{1,0:T(8,128)}) custom-call(s32[512]{0:T(512)} %pos_hbm.3, f32[512,128]{1,0:T(8,128)} %bitcast.4, bf16[4,128,128]{2,1,0:T(8,128)(2,1)} %get-tuple-element.16.cs_hbm), custom_call_target="tpu_custom_call" | custom-call | tf_op jit(solution)/shard_map/lattice/pallas_call | solution.py:135
  22.5 31.9 %collect.1 = (f32[512,128]{1,0:T(8,128)}, f32[16,4,8,128]{3,2,1,0:T(8,128)}, f32[16,4,8,128]{3,2,1,0:T(8,128)}, f32[2,2,4,2,4,4096]{5,4,3,2,1,0:T(4,128)}) custom-call(s32[512]{0:T(512)} %pos_hbm.3, f32[8448,128]{1,0:T(8,128)} %get-tuple-element.17.re_hbm, f32[8448,128]{1,0:T(8,128)} %get-tuple-element.18.im_hbm, f32[16,128,128]{2,1,0:T(8,128)} %pot_hbm.1, ...), custom_call_target="tpu_custom_call" | custom-call | tf_op jit(solution)/shard_map/collect/pallas_call | solution.py:510
  54.4 9.2 %rotate.1 = (bf16[2,512,4096]{2,1,0:T(8,128)(2,1)}, f32[512,128]{1,0:T(8,128)}) custom-call(f32[16,4,8,128]{3,2,1,0:T(8,128)} %get-tuple-element.22.coef_hbm, f32[16,4,8,128]{3,2,1,0:T(8,128)} %get-tuple-element.23.image_hbm, f32[512,128]{1,0:T(8,128)} %get-tuple-element.24.applied_hbm, f32[32,4,4096]{2,1,0:T(4,128)} %bitcast.3, bf16[2,512,4096]{2,1,0:T(8,128)(2,1)} %base_hbm.1), custom_call_target="tpu_custom_call" | custom-call | tf_op jit(solution)/shard_map/rotate/pallas_call | solution.py:256

commit v9 on v8

--- a/solution.py
+++ b/solution.py
@@ -312,8 +312,8 @@
             self.remote(step).wait_send()
 
 
-def pack_rows(flat_ref, pack_ref, n_pool):
-    for k in range(n_pool):
+def pack_rows(flat_ref, pack_ref, owners):
+    for k in owners:
         for j in range(4):
             pack_ref[k, j] = flat_ref[pl.ds(k * 4 + j, 8, 64), :]
 
@@ -372,7 +372,7 @@
              for part in range(2) for band in range(4)], axis=1)
     planes = Exchange("tg", n_tg, tg, sticks_ref, planes_ref, send_t, recv_t, own_sem.at[0])
     planes.start()
-    pack_rows(flat_ref, pack_ref, n_pool)
+    pack_rows(flat_ref, pack_ref, range(n_pool))
     planes.wait_recv()
     remote(ritz_hbm, col_hbm.at[before], send_r.at[0], recv_r.at[0], pool=up).wait_recv()
     remote(ritz_hbm, col_hbm.at[after], send_r.at[1], recv_r.at[1], pool=down).wait_recv()
@@ -435,8 +435,6 @@
         load.wait()
     x_transforms(1, pot_ref, ax_ref, bx_ref, re_ref, im_ref)
     y_transform_back(bx_ref, re_ref, im_ref, grid_ref)
-    coef = Exchange("pool", n_pool, pool, pack_hbm, coef_ref, send_c, recv_c, own_sem.at[2])
-    coef.start()
     for k, block in enumerate((z, before, after, across)):
         ritz(2 + k, other.at[block], other.at[block], next_y).wait_recv()
     on_core = ritz(10, other, other, next_core)
@@ -445,30 +443,49 @@
     loads[6].wait()
     loads[7].wait()
 
-    def gather(peer):
-        @pl.loop(0, 8)
-        def _(block):
-            base = pl.multiple_of(block * 8, 8)
-            cols_ref[peer, pl.ds(base, 8), :] = jnp.concatenate(
-                [grid_ref[pl.ds(pos_ref[peer * 64 + base + k], 1), :] for k in range(8)], axis=0)
-
-    back = Exchange("tg", n_tg, tg, cols_ref, returned_ref, send_t, recv_t, own_sem.at[0])
-    back.start(gather)
-    usable = usable_ref[...]
-    back.wait_recv()
-    rows = []
-    for band in range(4):
-        rows.append(jnp.concatenate(
-            [returned_ref[t, :, part * 64 + band * 16:part * 64 + band * 16 + 16]
-             for part in range(2) for t in range(n_tg)], axis=1))
-    res = dot(lanes3(jnp.concatenate(rows, axis=0)), table_ref[...])
-    for band in range(4):
-        for part in range(2):
-            at = (part * 4 + band) * 64
-            applied_ref[at:at + 64, :] = res[band * 64:(band + 1) * 64, part * 128:(part + 1) * 128] * usable
-    pack_rows(applied_ref, pack_ref, n_pool)
+    backs = [Exchange("tg", n_tg, tg, cols_ref.at[half], returned_ref.at[half], send_t.at[half], recv_t.at[half],
+                      own_sem.at[2 + half]) for half in range(2)]
+    for half in range(2):
+        def gather(peer):
+            for block in range(4):
+                first = peer * 64 + block // 2 * 32 + half * 16 + block % 2 * 8
+                cols_ref[half, peer, block * 8:block * 8 + 8, :] = jnp.concatenate(
+                    [grid_ref[pl.ds(pos_ref[first + k], 1), :] for k in range(8)], axis=0)
+
+        backs[half].start(gather)
+    coef = Exchange("pool", n_pool, pool, pack_hbm, coef_ref, send_c, recv_c, own_sem.at[0])
+    coef.start()
     image = Exchange("pool", n_pool, pool, pack_ref, image_ref, send_p, recv_p, own_sem.at[1])
-    image.start()
+    for half in range(2):
+        backs[half].wait_recv()
+        rows = []
+        for band in range(4):
+            rows.append(jnp.concatenate(
+                [returned_ref[half, t, :, part * 64 + band * 16:part * 64 + band * 16 + 16]
+                 for part in range(2) for t in range(n_tg)], axis=1))
+        res = dot(lanes3(jnp.concatenate(rows, axis=0)), table_ref[...])
+        for high in range(2):
+            slot = high * 32 + half * 16
+            usable = usable_ref[slot:slot + 16, :]
+            for band in range(4):
+                for part in range(2):
+                    at = (part * 4 + band) * 64 + slot
+                    row = band * 32 + high * 16
+                    applied_ref[at:at + 16, :] = res[row:row + 16, part * 128:(part + 1) * 128] * usable
+        owners = [high * 8 + half * 4 + k for high in range(2) for k in range(4)]
+        pack_rows(applied_ref, pack_ref, owners)
+        for step in range(8):
+            turn = lax.rem(pool + step, 8)
+            owner = turn // 4 * 8 + half * 4 + lax.rem(turn, 4)
+
+            @pl.when(owner != pool)
+            def _():
+                image.remote(lax.rem(owner + n_pool - pool, n_pool)).start()
+
+            @pl.when(owner == pool)
+            def _():
+                image.own().start()
+
     coef.wait_recv()
     for load in loads[8:]:
         load.wait()
@@ -477,7 +494,7 @@
         ritz(6 + k, own.at[block], theirs.at[block], next_core).wait_recv()
     ritz(10, other, ritz_ref.at[1 - y, 1 - core], next_core).wait_recv()
     image.wait_recv()
-    for exchange in (back, coef, image):
+    for exchange in backs + [coef, image]:
         exchange.wait_send()
     for copy in sent:
         copy.wait_send()
@@ -516,10 +533,10 @@
         scratch_shapes=[pltpu.SMEM(stick_pos.shape, jnp.int32), pltpu.VMEM(re.shape, F32), pltpu.VMEM(im.shape, F32),
                         pltpu.VMEM(pot.shape, F32), pltpu.VMEM(usable.shape, F32), pltpu.VMEM(cs.shape, BF16),
                         pltpu.VMEM((256, 768), BF16), pltpu.VMEM((256, 768), BF16), pltpu.VMEM((768, 256), BF16),
-                        pltpu.VMEM((16384, 128), F32), pltpu.VMEM((n_tg, 64, 128), F32),
-                        pltpu.VMEM((n_tg, 64, 128), F32), pltpu.VMEM(pack.shape, F32),
-                        dma((n_tg,)), dma((n_tg,)), dma((n_pool,)), dma((n_pool,)), dma((n_pool,)), dma((n_pool,)),
-                        dma((3,)), dma((11,)), dma((11,)), dma((11,))],
+                        pltpu.VMEM((16384, 128), F32), pltpu.VMEM((2, n_tg, 32, 128), F32),
+                        pltpu.VMEM((2, n_tg, 32, 128), F32), pltpu.VMEM(pack.shape, F32),
+                        dma((2, n_tg)), dma((2, n_tg)), dma((n_pool,)), dma((n_pool,)), dma((n_pool,)), dma((n_pool,)),
+                        dma((4,)), dma((11,)), dma((11,)), dma((11,))],
         compiler_params=pltpu.CompilerParams(collective_id=1, has_side_effects=True, vmem_limit_bytes=LIMIT),
         name="collect",
     )(stick_pos, re, im, pot, usable, cs, pack, col)

time: 63.9 us -> 62.4 us (0.977)
  Pallas kernels: 62.9 us -> 61.4 us
    pallas_call x1, Pallas kernels: 31.9 us -> 30.4 us  [collect(): pl.pallas_call(functools.partial(collect_kernel, n_tg, n_pool), out_shape...]
where the time goes in v9:
time: 62.4 us; the launch traced here: 62.3 us
  Pallas kernels  61.4 us (98%)
  between operations  0.81 us (1%)
    pallas_call x1, Pallas kernels, collect(): pl.pallas_call(functools.partial(collect_kernel, n_tg, n_pool), out_shape...  30.4 us
    pallas_call x1, Pallas kernels, spread(): pl.pallas_call(functools.partial(spread_kernel, n_tg, n_pool), out_shape=...  14.4 us
    pallas_call x1, Pallas kernels, rotate(): pl.pallas_call(rotate_kernel, out_shape=[jax.ShapeDtypeStruct(base.shape,...  9.22 us
    pallas_call x1, Pallas kernels, lattice(): pl.pallas_call(lattice_kernel, out_shape=[jax.ShapeDtypeStruct(size, F32)...  7.44 us

profile of v9, /device:TPU:1, one launch (start us, length us, event | category | flops | bytes accessed | tf_op | source)
XLA Modules:
  0.0 62.3 jit_solution(8522930384804341016)
XLA Ops:
  0.6 14.4 %spread.1 = (f32[8,64,128]{2,1,0:T(8,128)}, f32[16,4,8,128]{3,2,1,0:T(8,128)}, f32[64,128]{1,0:T(8,128)}, bf16[4,128,128]{2,1,0:T(8,128)(2,1)}, f32[4,2,4,4096]{3,2,1,0:T(4,128)}) custom-call(f32[2,4,64,128]{3,2,1,0:T(8,128)} %wave_hbm.1, s32[8]{0:T(128)} %count_hbm.1, f32[2,4,4096]{2,1,0:T(4,128)} %ritz_hbm.1), custom_call_target="tpu_custom_call" | custom-call | tf_op jit(solution)/shard_map/spread/pallas_call | solution.py:507
  15.0 7.4 %lattice.1 = (f32[8448,128]{1,0:T(8,128)}, f32[8448,128]{1,0:T(8,128)}) custom-call(s32[512]{0:T(512)} %pos_hbm.3, f32[512,128]{1,0:T(8,128)} %bitcast.4, bf16[4,128,128]{2,1,0:T(8,128)(2,1)} %get-tuple-element.16.cs_hbm), custom_call_target="tpu_custom_call" | custom-call | tf_op jit(solution)/shard_map/lattice/pallas_call | solution.py:135
  22.5 30.4 %collect.1 = (f32[512,128]{1,0:T(8,128)}, f32[16,4,8,128]{3,2,1,0:T(8,128)}, f32[16,4,8,128]{3,2,1,0:T(8,128)}, f32[2,2,4,2,4,4096]{5,4,3,2,1,0:T(4,128)}) custom-call(s32[512]{0:T(512)} %pos_hbm.3, f32[8448,128]{1,0:T(8,128)} %get-tuple-element.17.re_hbm, f32[8448,128]{1,0:T(8,128)} %get-tuple-element.18.im_hbm, f32[16,128,128]{2,1,0:T(8,128)} %pot_hbm.1, ...), custom_call_target="tpu_custom_call" | custom-call | tf_op jit(solution)/shard_map/collect/pallas_call | solution.py:527
  52.9 9.2 %rotate.1 = (bf16[2,512,4096]{2,1,0:T(8,128)(2,1)}, f32[512,128]{1,0:T(8,128)}) custom-call(f32[16,4,8,128]{3,2,1,0:T(8,128)} %get-tuple-element.22.coef_hbm, f32[16,4,8,128]{3,2,1,0:T(8,128)} %get-tuple-element.23.image_hbm, f32[512,128]{1,0:T(8,128)} %get-tuple-element.24.applied_hbm, f32[32,4,4096]{2,1,0:T(4,128)} %bitcast.3, bf16[2,512,4096]{2,1,0:T(8,128)(2,1)} %base_hbm.1), custom_call_target="tpu_custom_call" | custom-call | tf_op jit(solution)/shard_map/rotate/pallas_call | solution.py:256

commit v10 on v9

--- a/solution.py
+++ b/solution.py
@@ -435,11 +435,6 @@
         load.wait()
     x_transforms(1, pot_ref, ax_ref, bx_ref, re_ref, im_ref)
     y_transform_back(bx_ref, re_ref, im_ref, grid_ref)
-    for k, block in enumerate((z, before, after, across)):
-        ritz(2 + k, other.at[block], other.at[block], next_y).wait_recv()
-    on_core = ritz(10, other, other, next_core)
-    on_core.start()
-    sent.append(on_core)
     loads[6].wait()
     loads[7].wait()
 
@@ -455,6 +450,11 @@
         backs[half].start(gather)
     coef = Exchange("pool", n_pool, pool, pack_hbm, coef_ref, send_c, recv_c, own_sem.at[0])
     coef.start()
+    for k, block in enumerate((z, before, after, across)):
+        ritz(2 + k, other.at[block], other.at[block], next_y).wait_recv()
+    on_core = ritz(10, other, other, next_core)
+    on_core.start()
+    sent.append(on_core)
     image = Exchange("pool", n_pool, pool, pack_ref, image_ref, send_p, recv_p, own_sem.at[1])
     for half in range(2):
         backs[half].wait_recv()

time: 62.4 us -> 61.7 us (0.989)
  Pallas kernels: 61.4 us -> 60.7 us
    pallas_call x1, Pallas kernels: 30.4 us -> 29.6 us  [collect(): pl.pallas_call(functools.partial(collect_kernel, n_tg, n_pool), out_shape...]
where the time goes in v10:
time: 61.7 us; the launch traced here: 61.5 us
  Pallas kernels  60.7 us (98%)
  between operations  0.81 us (1%)
    pallas_call x1, Pallas kernels, collect(): pl.pallas_call(functools.partial(collect_kernel, n_tg, n_pool), out_shape...  29.6 us
    pallas_call x1, Pallas kernels, spread(): pl.pallas_call(functools.partial(spread_kernel, n_tg, n_pool), out_shape=...  14.4 us
    pallas_call x1, Pallas kernels, rotate(): pl.pallas_call(rotate_kernel, out_shape=[jax.ShapeDtypeStruct(base.shape,...  9.22 us
    pallas_call x1, Pallas kernels, lattice(): pl.pallas_call(lattice_kernel, out_shape=[jax.ShapeDtypeStruct(size, F32)...  7.44 us

profile of v10, /device:TPU:1, one launch (start us, length us, event | category | flops | bytes accessed | tf_op | source)
XLA Modules:
  0.0 61.5 jit_solution(895086249838558119)
XLA Ops:
  0.6 14.4 %spread.1 = (f32[8,64,128]{2,1,0:T(8,128)}, f32[16,4,8,128]{3,2,1,0:T(8,128)}, f32[64,128]{1,0:T(8,128)}, bf16[4,128,128]{2,1,0:T(8,128)(2,1)}, f32[4,2,4,4096]{3,2,1,0:T(4,128)}) custom-call(f32[2,4,64,128]{3,2,1,0:T(8,128)} %wave_hbm.1, s32[8]{0:T(128)} %count_hbm.1, f32[2,4,4096]{2,1,0:T(4,128)} %ritz_hbm.1), custom_call_target="tpu_custom_call" | custom-call | tf_op jit(solution)/shard_map/spread/pallas_call | solution.py:507
  15.0 7.4 %lattice.1 = (f32[8448,128]{1,0:T(8,128)}, f32[8448,128]{1,0:T(8,128)}) custom-call(s32[512]{0:T(512)} %pos_hbm.3, f32[512,128]{1,0:T(8,128)} %bitcast.4, bf16[4,128,128]{2,1,0:T(8,128)(2,1)} %get-tuple-element.16.cs_hbm), custom_call_target="tpu_custom_call" | custom-call | tf_op jit(solution)/shard_map/lattice/pallas_call | solution.py:135
  22.5 29.6 %collect.1 = (f32[512,128]{1,0:T(8,128)}, f32[16,4,8,128]{3,2,1,0:T(8,128)}, f32[16,4,8,128]{3,2,1,0:T(8,128)}, f32[2,2,4,2,4,4096]{5,4,3,2,1,0:T(4,128)}) custom-call(s32[512]{0:T(512)} %pos_hbm.3, f32[8448,128]{1,0:T(8,128)} %get-tuple-element.17.re_hbm, f32[8448,128]{1,0:T(8,128)} %get-tuple-element.18.im_hbm, f32[16,128,128]{2,1,0:T(8,128)} %pot_hbm.1, ...), custom_call_target="tpu_custom_call" | custom-call | tf_op jit(solution)/shard_map/collect/pallas_call | solution.py:527
  52.1 9.2 %rotate.1 = (bf16[2,512,4096]{2,1,0:T(8,128)(2,1)}, f32[512,128]{1,0:T(8,128)}) custom-call(f32[16,4,8,128]{3,2,1,0:T(8,128)} %get-tuple-element.22.coef_hbm, f32[16,4,8,128]{3,2,1,0:T(8,128)} %get-tuple-element.23.image_hbm, f32[512,128]{1,0:T(8,128)} %get-tuple-element.24.applied_hbm, f32[32,4,4096]{2,1,0:T(4,128)} %bitcast.3, bf16[2,512,4096]{2,1,0:T(8,128)(2,1)} %base_hbm.1), custom_call_target="tpu_custom_call" | custom-call | tf_op jit(solution)/shard_map/rotate/pallas_call | solution.py:256
